TPU v7x, 32 devices: a whole 2x2x4 slice. The times are simulated.
32 devices in a mesh: run: 2 (over y), particle: 4 (over z), space: 4 (over x, core).
Axes of the slice: x: 2, y: 2, z: 4, core: 2. Of those that a mesh axis runs over, the one named last changes fastest.
Arguments:
- state: float32 [8, 8, 64, 1024], P(('run', 'particle'), None, 'space'), parts along dimension 0, may hold values from -6 to 6
- ancestors: int32 [8], P('run'), parts along dimension 0, may hold values from 0 to 3, as said below
- noise: bfloat16 [8, 2, 64, 1024], P(('run', 'particle'), None, 'space'), parts along dimension 0, may hold values from -6 to 6
Outputs:
- analysis: float32 [8, 8, 64, 1024], P(('run', 'particle'), None, 'space'), parts along dimension 0
There are 2 independent parts, one for each index of `run`. A program takes and returns all parts, laid end to end along the dimension named above; each array names one. Nothing has to cross between parts.
Inputs may be any that keep to these rules, and one draw needn't show every extreme that they name: ancestors come from systematic resampling with uneven weights, slots shuffled: some particles fill several slots, others none; particles 0 and 3 always fill some slot.
All inputs are finite; a program needn't handle non-finite values.
Results may differ from a plain program's by a relative error of at most 0.00055.
Values may be sent and summed in bfloat16 or wider, within the bound.
No kernel may reach another device: no remote copies, remote signals or barrier semaphores. Data moves between devices by JAX's collectives and lax.ppermute only.
A program may use at most 64 MiB of HBM per device.

v0:
```python
import jax
import jax.numpy as jnp
from jax import lax
from jax.sharding import PartitionSpec as P


def extended(cells, sides, width):
    for axis, dim in sides:
        count = lax.axis_size(axis)
        ends = count - 1
        head = lax.slice_in_dim(cells, 0, width, axis=dim)
        tail = lax.slice_in_dim(cells, cells.shape[dim] - width, cells.shape[dim], axis=dim)
        cells = jnp.concatenate(
            [
                lax.ppermute(tail, axis, [(i, (i + 1) % count) for i in range(ends)]),
                cells,
                lax.ppermute(head, axis, [((i + 1) % count, i) for i in range(ends)]),
            ],
            axis=dim,
        )
    return cells


def split_levels(array):
    return array.reshape(array.shape[:-3] + (2, 4) + array.shape[-2:])


def advance(middle, below, above):
    row_total = middle.shape[-2]
    row_index = lax.broadcasted_iota(jnp.int32, (row_total, 1), 0)
    north = jnp.where(row_index == row_total - 1, above, jnp.roll(middle, -1, axis=-2))
    south = jnp.where(row_index == 0, below, jnp.roll(middle, 1, axis=-2))
    east = jnp.roll(middle, -1, axis=-1)
    west = jnp.roll(middle, 1, axis=-1)
    fields = split_levels(middle)
    grad_x = split_levels(0.5 * (east - west))
    grad_y = split_levels(0.5 * (north - south))
    laplace = split_levels(east + west + north + south - 4.0 * middle)
    speed_u = fields[..., 0, :, :]
    speed_v = fields[..., 1, :, :]
    height = fields[..., 2, :, :]
    passive_scalar = fields[..., 3, :, :]
    hx = grad_x[..., 2, :, :]
    hy = grad_y[..., 2, :, :]
    press_x = jnp.stack(
        [hx[..., 0, :, :] + hx[..., 1, :, :], hx[..., 0, :, :] + 1.6 * hx[..., 1, :, :]], axis=-3
    )
    press_y = jnp.stack(
        [hy[..., 0, :, :] + hy[..., 1, :, :], hy[..., 0, :, :] + 1.6 * hy[..., 1, :, :]], axis=-3
    )
    depth = jnp.array([0.8, 0.5], dtype=jnp.float32).reshape(2, 1, 1)
    new_u = speed_u + 0.3 * speed_v - 0.25 * press_x - 0.05 * speed_u + 0.1 * laplace[..., 0, :, :]
    new_v = speed_v - 0.3 * speed_u - 0.25 * press_y - 0.05 * speed_v + 0.1 * laplace[..., 1, :, :]
    new_h = (
        height - depth * (grad_x[..., 0, :, :] + grad_y[..., 1, :, :]) + 0.1 * laplace[..., 2, :, :]
    )
    new_q = (
        passive_scalar
        - 0.25 * (speed_u * grad_x[..., 3, :, :] + speed_v * grad_y[..., 3, :, :])
        + 0.1 * laplace[..., 3, :, :]
    )
    result = jnp.stack([new_u, new_v, new_h, new_q], axis=-3)
    return result.reshape(middle.shape)


def widen(field):
    return extended(field.astype(jnp.bfloat16), (("space", 2),), 1).astype(field.dtype)


def smooth(padded):
    middle = padded[..., 1:-1, :]
    total = 4.0 * middle + padded[..., 2:, :] + padded[..., :-2, :]
    total = total + jnp.roll(middle, -1, axis=-1) + jnp.roll(middle, 1, axis=-1)
    return 0.06 * total


def add_noise(resampled, smoothed):
    levels = split_levels(resampled)
    height = levels[:, :, 2:3] + smoothed[:, :, None]
    joined = jnp.concatenate([levels[:, :, :2], height, levels[:, :, 3:]], axis=2)
    return joined.reshape(resampled.shape)


def per_device(state, ancestors, noise):
    current = state
    for substep in range(2):
        padded = widen(current)
        current = advance(current, padded[..., :1, :], padded[..., -1:, :])
    local_count = current.shape[0]
    flat = current.reshape(local_count, current.shape[1], -1)
    cut_piece = lax.all_to_all(flat, "particle", split_axis=2, concat_axis=0, tiled=True)
    source_ids = jnp.arange(cut_piece.shape[0], dtype=jnp.int32)
    selection_mask = (ancestors[:, None] == source_ids[None, :]).astype(jnp.float32)
    picked_particle = jnp.einsum(
        "xi,izu->xzu", selection_mask, cut_piece, precision=lax.Precision.HIGHEST
    )
    moved = lax.all_to_all(picked_particle, "particle", split_axis=0, concat_axis=2, tiled=True)
    resampled = moved.reshape(current.shape)
    wide_noise = extended(noise, (("space", 2),), 1)
    smoothed = smooth(wide_noise.astype(jnp.float32))
    return add_noise(resampled, smoothed)


def solution(mesh):
    in_specs = (
        P(("run", "particle"), None, "space", None),
        P("run"),
        P(("run", "particle"), None, "space", None),
    )
    out_specs = P(("run", "particle"), None, "space", None)
    return jax.shard_map(
        per_device, mesh=mesh, in_specs=in_specs, out_specs=out_specs, check_vma=False
    )
```

profile of v0, /device:TPU:0, one launch (start us, length us, event | category | flops | bytes accessed | tf_op | source)
XLA Modules:
  0.0 207.7 jit_solution(10355673611594590616)
XLA Ops:
  0.0 1.4 copy.453
  2.0 2.3 %collective-permute-start = (bf16[1,8,1,1024]{3,1,2,0:T(8,128)(2,1)}, bf16[1,8,1,1024]{3,1,2,0:T(8,128)(2,1)S(1)}, u32[]{:S(2)}, u32[]{:S(2)}) collective-permute-start(bf16[1,8,1,1024]{3,1,2,0:T(8,128)(2,1)} %get-tuple-element.45), channel_id=1, source_target_pairs={{0,1},{1,2},{2,3},{4,5},{5,6},{6,7},{8,9},{9,10},{10,11},{12,13},{... | collective-permute-start | bytes 49160 | tf_op jit(solution)/shard_map/ppermute | solution.py:15
  4.4 1.3 collective-permute-start.1
  5.7 1.3 fusion.57
  8.1 1.6 slice_reduce_fusion.2
  9.6 1.4 fusion.58
  12.8 1.9 fusion
  17.4 1.2 fusion.3
  25.7 5.7 %collective-permute-start.2 = (bf16[1,8,1,1024]{3,1,2,0:T(8,128)(2,1)S(1)}, bf16[1,8,1,1024]{3,1,2,0:T(8,128)(2,1)}, u32[]{:S(2)}, u32[]{:S(2)}) collective-permute-start(bf16[1,8,1,1024]{3,1,2,0:T(8,128)(2,1)S(1)} %copy.410), channel_id=1, source_target_pairs={{0,1},{1,2},{2,3},{4,5},{5,6},{6,7},{8,9},{9,10},{10,11},{12,13},{... | collective-permute-start | bytes 49160 | tf_op jit(solution)/shard_map/ppermute | solution.py:15
  32.1 1.3 collective-permute-start.3
  33.4 1.4 concatenate.323
  35.9 1.4 concatenate.327
  44.9 12.0 %copy.428 = f32[1,8,16384]{1,0,2:T(1,128)} copy(f32[1,8,16384]{2,1,0:T(8,128)S(1)} %reshape_reshape.6) | data formatting | bytes 1048576 | tf_op jit(solution)/shard_map/reshape;reshape | solution.py:90
  57.5 74.5 %reduce.12 = f32[16384,8]{1,0:T(8,128)} reduce(f32[16384,1,8]{2,1,0:T(1,128)} %bitcast.180, f32[]{:T(128)} %broadcast.427), dimensions={1}, to_apply=%bitcast.178.reduce_sub_computation | reduce | bytes 1048580
  131.9 6.6 %reshape.1179 = f32[4,1,32768]{2,1,0:T(1,128)S(1)} reshape(f32[16384,8]{1,0:T(8,128)} %reduce.12) | data formatting | bytes 1048576
  138.5 20.1 %all_to_all.33 = f32[4,1,32768]{2,1,0:T(1,128)S(1)} all-to-all(f32[4,1,32768]{2,1,0:T(1,128)S(1)} %reshape.1179), channel_id=1, replica_groups=mesh['run'=2,'particle'=4,'space'=4] {'particle'}, dimensions={0} | all-to-all | bytes 1048576 | tf_op jit(solution)/shard_map/all_to_all | solution.py:91
  158.6 2.1 %reduce.13 = f32[4,32768]{1,0:T(4,128)S(1)} reduce(f32[4,1,32768]{2,1,0:T(1,128)S(1)} %all_to_all.33, f32[]{:T(128)} %broadcast.427), dimensions={1}, to_apply=%all_to_all.24.reduce_sub_computation | reduce | bytes 1048580 | tf_op jit(solution)/shard_map/all_to_all | solution.py:91
  160.8 19.8 %reshape.1180 = f32[16384,1,8]{2,1,0:T(1,128)} reshape(f32[4,32768]{1,0:T(4,128)S(1)} %reduce.13) | data formatting | bytes 1048576
  180.6 5.2 %copy.432 = f32[1,8,4,4096]{3,2,1,0:T(4,128)S(1)} copy(f32[1,8,4,4096]{1,3,2,0:T(8,128)} %bitcast.181) | data formatting | bytes 1048576 | tf_op jit(solution)/shard_map/all_to_all | solution.py:91
  187.5 3.5 %all-to-all-start.1 = ((f32[4,8,4096]{2,1,0:T(8,128)}), f32[4,8,4096]{2,1,0:T(8,128)S(1)}, u32[]{:S(2)}, u32[]{:S(2)}) async-start(f32[4,8,4096]{2,1,0:T(8,128)} %copy.430), calls=%async_computation.1 | async-start | bytes 1048576 | tf_op jit(solution)/shard_map/all_to_all | solution.py:97
  191.0 2.2 %collective-permute-start.4 = (bf16[1,2,1,1024]{3,2,1,0:T(2,128)(2,1)S(1)}, bf16[1,2,1,1024]{3,2,1,0:T(2,128)(2,1)S(1)}, u32[]{:S(2)}, u32[]{:S(2)}) collective-permute-start(bf16[1,2,1,1024]{3,2,1,0:T(2,128)(2,1)S(1)} %get-tuple-element.59), channel_id=1, source_target_pairs={{0,1},{1,2},{2,3},{4,5},{5,6},{6,7},{8,9},{9,10},{10,11},{12,13},{... | collective-permute-start | bytes 12296 | tf_op jit(solution)/shard_map/ppermute | solution.py:15
  193.2 1.3 collective-permute-start.5
  194.5 3.1 %collective-permute-done.5 = bf16[1,2,1,1024]{3,2,1,0:T(2,128)(2,1)S(1)} collective-permute-done((bf16[1,2,1,1024]{3,2,1,0:T(2,128)(2,1)S(1)}, bf16[1,2,1,1024]{3,2,1,0:T(2,128)(2,1)S(1)}, u32[]{:S(2)}, u32[]{:S(2)}) %collective-permute-start.5) | collective-permute-done | bytes 4128 | tf_op jit(solution)/shard_map/ppermute | solution.py:17
  197.8 8.4 %all-to-all-done.1 = f32[4,8,4096]{2,1,0:T(8,128)S(1)} async-done(((f32[4,8,4096]{2,1,0:T(8,128)}), f32[4,8,4096]{2,1,0:T(8,128)S(1)}, u32[]{:S(2)}, u32[]{:S(2)}) %all-to-all-start.1) | async-done | bytes 524320 | tf_op jit(solution)/shard_map/all_to_all | solution.py:97
  (75 shorter events, 26.6 us)
Async XLA Ops:
  0.0 17.4 %copy-start = (f32[1,8,16,1024]{3,2,1,0:T(8,128)S(1)}, f32[1,8,16,1024]{3,2,1,0:T(8,128)}, u32[]{:S(2)}) copy-start(f32[1,8,16,1024]{3,2,1,0:T(8,128)} %param.5) | copy-start | bytes 1572868
  2.0 13.3 %collective-permute-start = (bf16[1,8,1,1024]{3,1,2,0:T(8,128)(2,1)}, bf16[1,8,1,1024]{3,1,2,0:T(8,128)(2,1)S(1)}, u32[]{:S(2)}, u32[]{:S(2)}) collective-permute-start(bf16[1,8,1,1024]{3,1,2,0:T(8,128)(2,1)} %get-tuple-element.45), channel_id=1, source_target_pairs={{0,1},{1,2},{2,3},{4,5},{5,6},{6,7},{8,9},{9,10},{10,11},{12,13},{... | collective-permute-start | bytes 49160 | tf_op jit(solution)/shard_map/ppermute | solution.py:15
  4.4 10.9 %collective-permute-start.1 = (bf16[1,8,1,1024]{3,1,2,0:T(8,128)(2,1)}, bf16[1,8,1,1024]{3,1,2,0:T(8,128)(2,1)}, u32[]{:S(2)}, u32[]{:S(2)}) collective-permute-start(bf16[1,8,1,1024]{3,1,2,0:T(8,128)(2,1)} %get-tuple-element.46), channel_id=1, source_target_pairs={{1,0},{2,1},{3,2},{5,4},{6,5},{7,6},{9,8},{10,9},{11,10},{13,12},{... | collective-permute-start | bytes 49160 | tf_op jit(solution)/shard_map/ppermute | solution.py:17
  23.2 0.8 copy-start.1
  25.7 12.7 %collective-permute-start.2 = (bf16[1,8,1,1024]{3,1,2,0:T(8,128)(2,1)S(1)}, bf16[1,8,1,1024]{3,1,2,0:T(8,128)(2,1)}, u32[]{:S(2)}, u32[]{:S(2)}) collective-permute-start(bf16[1,8,1,1024]{3,1,2,0:T(8,128)(2,1)S(1)} %copy.410), channel_id=1, source_target_pairs={{0,1},{1,2},{2,3},{4,5},{5,6},{6,7},{8,9},{9,10},{10,11},{12,13},{... | collective-permute-start | bytes 49160 | tf_op jit(solution)/shard_map/ppermute | solution.py:15
  32.1 7.1 %collective-permute-start.3 = (bf16[1,8,1,1024]{3,1,2,0:T(8,128)(2,1)}, bf16[1,8,1,1024]{3,1,2,0:T(8,128)(2,1)}, u32[]{:S(2)}, u32[]{:S(2)}) collective-permute-start(bf16[1,8,1,1024]{3,1,2,0:T(8,128)(2,1)} %copy.412), channel_id=1, source_target_pairs={{1,0},{2,1},{3,2},{5,4},{6,5},{7,6},{9,8},{10,9},{11,10},{13,12},{... | collective-permute-start | bytes 49160 | tf_op jit(solution)/shard_map/ppermute | solution.py:17
  160.8 24.9 %copy-start.3 = (s32[4]{0:T(128)S(1)}, s32[4]{0:T(128)}, u32[]{:S(2)}) copy-start(s32[4]{0:T(128)} %param.6) | copy-start | bytes 52
  160.8 30.2 %copy-start.2 = (bf16[1,2,16,1024]{3,2,1,0:T(8,128)(2,1)S(1)}, bf16[1,2,16,1024]{3,2,1,0:T(8,128)(2,1)}, u32[]{:S(2)}) copy-start(bf16[1,2,16,1024]{3,2,1,0:T(8,128)(2,1)} %param.7) | copy-start | bytes 196612
  187.5 18.7 %all-to-all-start.1 = ((f32[4,8,4096]{2,1,0:T(8,128)}), f32[4,8,4096]{2,1,0:T(8,128)S(1)}, u32[]{:S(2)}, u32[]{:S(2)}) async-start(f32[4,8,4096]{2,1,0:T(8,128)} %copy.430), calls=%async_computation.1 | async-start | bytes 1048576 | tf_op jit(solution)/shard_map/all_to_all | solution.py:97
  191.0 3.5 %collective-permute-start.4 = (bf16[1,2,1,1024]{3,2,1,0:T(2,128)(2,1)S(1)}, bf16[1,2,1,1024]{3,2,1,0:T(2,128)(2,1)S(1)}, u32[]{:S(2)}, u32[]{:S(2)}) collective-permute-start(bf16[1,2,1,1024]{3,2,1,0:T(2,128)(2,1)S(1)} %get-tuple-element.59), channel_id=1, source_target_pairs={{0,1},{1,2},{2,3},{4,5},{5,6},{6,7},{8,9},{9,10},{10,11},{12,13},{... | collective-permute-start | bytes 12296 | tf_op jit(solution)/shard_map/ppermute | solution.py:15
  193.2 4.4 %collective-permute-start.5 = (bf16[1,2,1,1024]{3,2,1,0:T(2,128)(2,1)S(1)}, bf16[1,2,1,1024]{3,2,1,0:T(2,128)(2,1)S(1)}, u32[]{:S(2)}, u32[]{:S(2)}) collective-permute-start(bf16[1,2,1,1024]{3,2,1,0:T(2,128)(2,1)S(1)} %get-tuple-element.60), channel_id=1, source_target_pairs={{1,0},{2,1},{3,2},{5,4},{6,5},{7,6},{9,8},{10,9},{11,10},{13,12},{... | collective-permute-start | bytes 12296 | tf_op jit(solution)/shard_map/ppermute | solution.py:17
where the time goes:
time: 209 us; the launch traced here: 208 us
  other arithmetic  91.3 us (44%)
  local copies, waits for them, and re-layouts  66.2 us (32%)
  blocking collectives  20.1 us (10%)
  starting transfers between devices  17.6 us (8%)
  waiting for transfers between devices  11.4 us (5%)
    unnamed x1, other arithmetic  74.5 us
    unnamed x12, local copies, waits for them, and re-layouts  29.1 us
    all_to_all x1, blocking collectives, per_device(): lax.all_to_all(flat, 'particle', split_axis=2, concat_axis=0, tiled=True)  20.1 us
    another operation x2, local copies, waits for them, and re-layouts, per_device(): flat = current.reshape(local_count, current.shape[1], -1)  12.1 us
    ppermute x3, starting transfers between devices, extended(): lax.ppermute(tail, axis, [(i, (i + 1) % count) for i in range(ends)])  10.3 us
    all_to_all x1, waiting for transfers between devices, per_device(): lax.all_to_all(picked_particle, 'particle', split_axis=0, concat_axis=2,...  8.36 us
    all_to_all x1, local copies, waits for them, and re-layouts, per_device(): lax.all_to_all(flat, 'particle', split_axis=2, concat_axis=0, tiled=True)  5.15 us
  transfers between devices with their start and end apart: 7, of which 2 were waited for; matrix products, arithmetic and copies ran while one was open for 8% of the time, Pallas kernels for 0%

commit v1 on v0

v1 whole, which is shorter than its diff:
```python
import functools

import jax
import jax.numpy as jnp
from jax import lax
from jax.experimental import pallas as pl
from jax.experimental.pallas import tpu as pltpu
from jax.sharding import PartitionSpec as P

SCALE = 8192.0
WIRE = jnp.float16
DEPTHS = (0.8, 0.5)
SECOND = (1.0, 1.6)


def pack(values):
    return (values.astype(jnp.float32) * SCALE).astype(WIRE)


def unpack(values):
    return values.astype(jnp.float32) * (1.0 / SCALE)


def lane_roll(a, shift):
    return pltpu.roll(a, shift % a.shape[-1], a.ndim - 1)


def row_roll(a, shift):
    return pltpu.roll(a, shift % a.shape[-2], a.ndim - 2)


def neighbours(a, below=None, above=None):
    east, west = lane_roll(a, -1), lane_roll(a, 1)
    north, south = row_roll(a, -1), row_roll(a, 1)
    if below is not None:
        rows = a.shape[0]
        index = lax.broadcasted_iota(jnp.int32, a.shape, 0)
        north = jnp.where(index == rows - 1, above, north)
        south = jnp.where(index == 0, below, south)
    return east, west, north, south


def advance(fields, below=None, above=None):
    around = [
        neighbours(f, *((below[i], above[i]) if below is not None else ()))
        for i, f in enumerate(fields)
    ]
    out = []
    hx = [around[l * 4 + 2][0] - around[l * 4 + 2][1] for l in range(2)]
    hy = [around[l * 4 + 2][2] - around[l * 4 + 2][3] for l in range(2)]
    for l in range(2):
        u, v, h, q = fields[l * 4 : l * 4 + 4]
        eu, wu, nu, su = around[l * 4]
        ev, wv, nv, sv = around[l * 4 + 1]
        eh, wh, nh, sh = around[l * 4 + 2]
        eq, wq, nq, sq = around[l * 4 + 3]
        px = hx[0] + SECOND[l] * hx[1]
        py = hy[0] + SECOND[l] * hy[1]
        out.append(0.55 * u + 0.3 * v - 0.125 * px + 0.1 * (eu + wu + nu + su))
        out.append(0.55 * v - 0.3 * u - 0.125 * py + 0.1 * (ev + wv + nv + sv))
        out.append(
            0.6 * h
            - (0.5 * DEPTHS[l]) * ((eu - wu) + (nv - sv))
            + 0.1 * (eh + wh + nh + sh)
        )
        out.append(
            0.6 * q
            - 0.125 * (u * (eq - wq) + v * (nq - sq))
            + 0.1 * (eq + wq + nq + sq)
        )
    return out


def finish_kernel(parts, place_ref, *refs):
    piece_refs, (pair_ref, other_ref, noise_ref, out_ref, held, edge) = (
        refs[:parts],
        refs[parts:],
    )
    me = place_ref[0]
    even = place_ref[1] == 0
    width = held.shape[0] // parts
    fields_total, rows, cols = held.shape
    for m in range(parts):
        spot = pl.ds((me ^ m) * width, width)
        held[spot] = piece_refs[m][...]
        old = pl.ds(m * width, width)
        edge[0, spot] = jnp.where(even, other_ref[old], pair_ref[old])
        edge[1, spot] = jnp.where(even, pair_ref[old], other_ref[old])
    scale = 1.0 / SCALE
    fields = [held[f] for f in range(fields_total)]
    lower = [edge[0, f] * scale for f in range(fields_total)]
    upper = [edge[1, f] * scale for f in range(fields_total)]
    strip = [
        jnp.concatenate(
            [lower[f], fields[f][:1], fields[f][rows - 1 :], upper[f], upper[f]], axis=0
        )
        for f in range(fields_total)
    ]
    strip = advance(strip)
    first = advance(
        fields, [e[1:2] for e in lower], [e[0:1] for e in upper]
    )
    keep_low = jnp.where(place_ref[2] == 1, 0.0, 1.0)
    keep_high = jnp.where(place_ref[3] == 1, 0.0, 1.0)
    second = advance(
        first, [s[1:2] * keep_low for s in strip], [s[4:5] * keep_high for s in strip]
    )
    for f in range(fields_total):
        if f % 4 != 2:
            out_ref[f] = second[f]
    pair_noise = pair_ref[fields_total] * scale
    other_noise = other_ref[fields_total] * scale
    below = jnp.where(even, other_noise, pair_noise)
    above = jnp.where(even, pair_noise, other_noise)
    for l in range(2):
        n = noise_ref[l].astype(jnp.float32)
        e, w, no, so = neighbours(n, below[l : l + 1], above[l : l + 1])
        out_ref[l * 4 + 2] = second[l * 4 + 2] + 0.06 * (4.0 * n + e + w + no + so)


def finish(place, pieces, pair, other, noise):
    parts = len(pieces)
    fields = parts * pieces[0].shape[0]
    rows, cols = pieces[0].shape[1:]
    vmem = pl.BlockSpec(memory_space=pltpu.VMEM)
    return pl.pallas_call(
        functools.partial(finish_kernel, parts),
        out_shape=jax.ShapeDtypeStruct((fields, rows, cols), jnp.float32),
        in_specs=[pl.BlockSpec(memory_space=pltpu.SMEM)] + [vmem] * (parts + 3),
        out_specs=vmem,
        scratch_shapes=[
            pltpu.VMEM((fields, rows, cols), jnp.float32),
            pltpu.VMEM((2, fields, 2, cols), jnp.float32),
        ],
        compiler_params=pltpu.CompilerParams(vmem_limit_bytes=32 * 1024 * 1024),
        cost_estimate=pl.CostEstimate(
            flops=130 * fields * rows * cols, bytes_accessed=1 << 20, transcendentals=0
        ),
    )(place, *pieces, pair, other, noise)


def fetch_by_permutes(state, ancestors, count, me):
    def swap(a, m):
        return lax.ppermute(a, "particle", [(i, i ^ m) for i in range(count)])

    fields, rows, cols = state.shape
    cut = state.reshape(count, fields // count, rows, cols)

    def part(m):
        return pack(lax.dynamic_index_in_dim(cut, me ^ m, 0, keepdims=False))

    here = [part(0)] + [swap(part(m), m) for m in range(1, count)]

    def pick(slot):
        which = lax.dynamic_index_in_dim(ancestors, slot, 0, keepdims=False) ^ me
        chosen = here[0]
        for m in range(1, count):
            chosen = jnp.where(which == m, here[m], chosen)
        return chosen

    return [pick(me)] + [swap(pick(me ^ m), m) for m in range(1, count)]


def fetch_by_all_to_all(state, ancestors, count):
    fields, rows, cols = state.shape
    cut = pack(state).reshape(fields, rows, count, cols // count).transpose(2, 0, 1, 3)
    here = lax.all_to_all(cut, "particle", split_axis=0, concat_axis=0, tiled=True)
    chosen = jnp.take(here, ancestors, axis=0)
    back = lax.all_to_all(chosen, "particle", split_axis=0, concat_axis=0, tiled=True)
    return back.transpose(1, 2, 0, 3).reshape(fields, rows, cols)


def per_device(state, ancestors, noise):
    state, noise = state[0], noise[0]
    count = lax.axis_size("particle")
    me = lax.axis_index("particle")
    if count in (2, 4, 8):
        order = me
        pieces = fetch_by_permutes(state, ancestors, count, me)
    else:
        order = jnp.int32(0)
        pieces = [fetch_by_all_to_all(state, ancestors, count)]

    blocks = lax.axis_size("space")
    where = lax.axis_index("space")
    even = where % 2 == 0
    low = jnp.concatenate(
        [p[:, :2] for p in pieces] + [pack(noise[:, :1]).reshape(1, 2, -1)], axis=0
    )
    high = jnp.concatenate(
        [p[:, -2:] for p in pieces] + [pack(noise[:, -1:]).reshape(1, 2, -1)], axis=0
    )
    pairs = [(i, i ^ 1) for i in range(blocks)]
    others = [
        p for i in range(1, blocks - 1, 2) for p in ((i, i + 1), (i + 1, i))
    ]
    pair = lax.ppermute(jnp.where(even, high, low), "space", pairs)
    other = lax.ppermute(jnp.where(even, low, high), "space", others)

    place = jnp.stack(
        [order, where % 2, (where == 0).astype(jnp.int32), (where == blocks - 1).astype(jnp.int32)]
    ).astype(jnp.int32)
    out = finish(
        place,
        [unpack(p) for p in pieces],
        pair.astype(jnp.float32),
        other.astype(jnp.float32),
        noise,
    )
    return out[None]


def solution(mesh):
    in_specs = (
        P(("run", "particle"), None, "space", None),
        P("run"),
        P(("run", "particle"), None, "space", None),
    )
    out_specs = P(("run", "particle"), None, "space", None)
    return jax.shard_map(
        per_device, mesh=mesh, in_specs=in_specs, out_specs=out_specs, check_vma=False
    )
```

time: 209 us -> 29.1 us (0.14)
  other arithmetic: 91.3 us -> 2.43 us
  local copies, waits for them, and re-layouts: 66.2 us -> 0.79 us
  blocking collectives: 20.1 us -> 0 us
  waiting for transfers between devices: 11.4 us -> 6.37 us
  starting transfers between devices: 17.6 us -> 13.8 us
  Pallas kernels: 0 us -> 2.46 us
  between operations: 0.42 us -> 2.69 us
    unnamed x1 -> x0, other arithmetic: 74.5 us -> none
    unnamed x12 -> x8, local copies, waits for them, and re-layouts: 29.1 us -> 0.12 us
    all_to_all x1 -> x0, blocking collectives: 20.1 us -> none  [per_device(): lax.all_to_all(flat, 'particle', split_axis=2, concat_axis=0, tiled=True)]
    another operation x4 -> x0, local copies, waits for them, and re-layouts: 12.4 us -> none  [the longest x2 12.1 us: per_device(): flat = current.reshape(local_count, current.shape[1], -1)]
    slice x15 -> x0, local copies, waits for them, and re-layouts: 8.85 us -> none  [the longest x2 2.98 us: advance(): west = jnp.roll(middle, 1, axis=-1)]
    all_to_all x1 -> x0, waiting for transfers between devices: 8.36 us -> none  [per_device(): lax.all_to_all(picked_particle, 'particle', split_axis=0, concat_axis=2,...]
    concatenate x8 -> x1, local copies, waits for them, and re-layouts: 6.09 us -> 0.02 us  [per_device(): jnp.concatenate([p[:, -2:] for p in pieces] + [pack(noise[:, -1:]).reshap...]
    all_to_all x2 -> x0, local copies, waits for them, and re-layouts: 5.49 us -> none  [the longest x1 5.15 us: per_device(): lax.all_to_all(flat, 'particle', split_axis=2, concat_axis=0, tiled=True)]
  transfers between devices with their start and end apart: 7 -> 8, of which waited for: 2 -> 5; matrix products, arithmetic and copies ran while one was open for 8% -> 4% of each run, Pallas kernels for 0% -> 0%
where the time goes in v1:
time: 29.1 us; the launch traced here: 28.6 us
  starting transfers between devices  13.8 us (47%)
  waiting for transfers between devices  6.37 us (22%)
  between operations  2.69 us (9%)
  Pallas kernels  2.46 us (8%)
  other arithmetic  2.43 us (8%)
  local copies, waits for them, and re-layouts  0.79 us (3%)
    ppermute x6, starting transfers between devices, swap(): return lax.ppermute(a, 'particle', [(i, i ^ m) for i in range(count)])  10.3 us
    ppermute x6, waiting for transfers between devices, swap(): return lax.ppermute(a, 'particle', [(i, i ^ m) for i in range(count)])  5.61 us
    ppermute x1, starting transfers between devices, per_device(): pair = lax.ppermute(jnp.where(even, high, low), 'space', pairs)  2.92 us
    pallas_call x1, Pallas kernels, finish(): pl.pallas_call(functools.partial(finish_kernel, parts), out_shape=jax.Sha...  2.46 us
    convert_element_type x2, other arithmetic, pack(): return (values.astype(jnp.float32) * SCALE).astype(WIRE)  1.11 us
    select_n x2, other arithmetic, pick(): chosen = jnp.where(which == m, here[m], chosen)  1.01 us
    ppermute x1, waiting for transfers between devices, per_device(): pair = lax.ppermute(jnp.where(even, high, low), 'space', pairs)  0.76 us
    ppermute x1, starting transfers between devices, per_device(): other = lax.ppermute(jnp.where(even, low, high), 'space', others)  0.66 us
  transfers between devices with their start and end apart: 8, of which 5 were waited for; matrix products, arithmetic and copies ran while one was open for 4% of the time, Pallas kernels for 0%

profile of v1, /device:TPU:0, one launch (start us, length us, event | category | flops | bytes accessed | tf_op | source)
XLA Modules:
  0.0 28.6 jit_solution(5733171597552915158)
XLA Ops:
  0.0 1.1 %fusion.2 = (f16[2,16,1024]{2,1,0:T(8,128)(2,1)S(1)}, f16[2,16,1024]{2,1,0:T(8,128)(2,1)S(1)}, f16[2,16,1024]{2,1,0:T(8,128)(2,1)S(1)}) fusion(f32[4,2,16,1024]{3,2,1,0:T(8,128)} %bitcast.26, s32[]{:T(128)S(6)} %select_n.120, s32[]{:T(128)S(6)} %select_n.118, s32[]{:T(128)S(6)} %select_n.116), kind=kLoop, calls=%fused_computation.12 | loop fusion | flops 196608 | bytes 589836 | tf_op jit(solution)/shard_map/convert_element_type | solution.py:17
  1.1 0.0 copy-start
  1.1 3.1 %collective-permute-start.2 = (f16[2,16,1024]{2,1,0:T(8,128)(2,1)S(1)}, f16[2,16,1024]{2,1,0:T(8,128)(2,1)S(1)}, u32[]{:S(2)}, u32[]{:S(2)}) collective-permute-start(f16[2,16,1024]{2,1,0:T(8,128)(2,1)S(1)} %get-tuple-element.9), channel_id=1, source_target_pairs={{0,4},{4,0},{8,12},{12,8},{1,5},{5,1},{9,13},{13,9},{2,6},{6,2},{1... | collective-permute-start | bytes 196616 | tf_op jit(solution)/shard_map/ppermute | solution.py:144
  4.2 2.6 %collective-permute-start.1 = (f16[2,16,1024]{2,1,0:T(8,128)(2,1)S(1)}, f16[2,16,1024]{2,1,0:T(8,128)(2,1)S(1)}, u32[]{:S(2)}, u32[]{:S(2)}) collective-permute-start(f16[2,16,1024]{2,1,0:T(8,128)(2,1)S(1)} %get-tuple-element.10), channel_id=1, source_target_pairs={{0,8},{4,12},{8,0},{12,4},{1,9},{5,13},{9,1},{13,5},{2,10},{6,14},... | collective-permute-start | bytes 196616 | tf_op jit(solution)/shard_map/ppermute | solution.py:144
  6.8 0.0 collective-permute-start
  6.8 0.7 %fusion.9 = (s32[1]{0:T(128)}, s32[1]{0:T(128)}, s32[1]{0:T(128)}, s32[1]{0:T(128)}) fusion(s32[4]{0:T(128)S(1)} %copy-done.1, s32[]{:T(128)S(6)} %select_n.118, s32[]{:T(128)S(6)} %select_n.120, s32[]{:T(128)S(6)} %select_n.114, s32[]{:T(128)S(6)} %select_n.116), kind=kLoop, calls=%fused_computation.35 | loop fusion | bytes 48 | tf_op jit(solution)/shard_map/jit(dynamic_index_in_dim)/dynamic_slice | solution.py:155
  10.0 0.1 pad_add_fusion.place_ref
  10.1 0.0 collective-permute-done.2
  10.1 1.3 %collective-permute-done.1 = f16[2,16,1024]{2,1,0:T(8,128)(2,1)S(1)} collective-permute-done((f16[2,16,1024]{2,1,0:T(8,128)(2,1)S(1)}, f16[2,16,1024]{2,1,0:T(8,128)(2,1)S(1)}, u32[]{:S(2)}, u32[]{:S(2)}) %collective-permute-start.1) | collective-permute-done | bytes 65568 | tf_op jit(solution)/shard_map/ppermute | solution.py:144
  11.4 1.4 %collective-permute-done = f16[2,16,1024]{2,1,0:T(8,128)(2,1)S(1)} collective-permute-done((f16[2,16,1024]{2,1,0:T(8,128)(2,1)S(1)}, f16[2,16,1024]{2,1,0:T(8,128)(2,1)S(1)}, u32[]{:S(2)}, u32[]{:S(2)}) %collective-permute-start) | collective-permute-done | bytes 65568 | tf_op jit(solution)/shard_map/ppermute | solution.py:144
  12.9 1.0 %select_select_fusion = (f16[2,16,1024]{2,1,0:T(8,128)(2,1)S(1)}, f16[2,16,1024]{2,1,0:T(8,128)(2,1)S(1)}) fusion(f16[2,16,1024]{2,1,0:T(8,128)(2,1)S(1)} %collective-permute-done, f16[2,16,1024]{2,1,0:T(8,128)(2,1)S(1)} %collective-permute-done.1, f16[2,16,1024]{2,1,0:T(8,128)(2,1)S(1)} %collective-permute-done.2, pred[]{:T(512)S(6)} %eq.61, pred[]{:T(512)S(6)} %eq.60, ...), kind=kLoop, calls=%fused_computation.14 | loop fusion | flops 163840 | bytes 458759 | tf_op jit(solution)/shard_map/jit(_where)/select_n | solution.py:158
  13.8 1.8 %collective-permute-start.5 = (f16[2,16,1024]{2,1,0:T(8,128)(2,1)S(1)}, f16[2,16,1024]{2,1,0:T(8,128)(2,1)S(1)}, u32[]{:S(2)}, u32[]{:S(2)}) collective-permute-start(f16[2,16,1024]{2,1,0:T(8,128)(2,1)S(1)} %get-tuple-element.5), channel_id=1, source_target_pairs={{0,12},{4,8},{8,4},{12,0},{1,13},{5,9},{9,5},{13,1},{2,14},{6,10},... | collective-permute-start | bytes 196616 | tf_op jit(solution)/shard_map/ppermute | solution.py:144
  15.7 0.1 select_select_fusion.1
  15.7 0.4 %collective-permute-start.3 = (f16[2,16,1024]{2,1,0:T(8,128)(2,1)S(1)}, f16[2,16,1024]{2,1,0:T(8,128)(2,1)S(1)}, u32[]{:S(2)}, u32[]{:S(2)}) collective-permute-start(f16[2,16,1024]{2,1,0:T(8,128)(2,1)S(1)} %get-tuple-element.13), channel_id=1, source_target_pairs={{0,4},{4,0},{8,12},{12,8},{1,5},{5,1},{9,13},{13,9},{2,6},{6,2},{1... | collective-permute-start | bytes 196616 | tf_op jit(solution)/shard_map/ppermute | solution.py:144
  16.2 2.3 %collective-permute-start.4 = (f16[2,16,1024]{2,1,0:T(8,128)(2,1)S(1)}, f16[2,16,1024]{2,1,0:T(8,128)(2,1)S(1)}, u32[]{:S(2)}, u32[]{:S(2)}) collective-permute-start(f16[2,16,1024]{2,1,0:T(8,128)(2,1)S(1)} %get-tuple-element.12), channel_id=1, source_target_pairs={{0,8},{4,12},{8,0},{12,4},{1,9},{5,13},{9,1},{13,5},{2,10},{6,14},... | collective-permute-start | bytes 196616 | tf_op jit(solution)/shard_map/ppermute | solution.py:144
  18.5 2.1 %collective-permute-done.3 = f16[2,16,1024]{2,1,0:T(8,128)(2,1)S(1)} collective-permute-done((f16[2,16,1024]{2,1,0:T(8,128)(2,1)S(1)}, f16[2,16,1024]{2,1,0:T(8,128)(2,1)S(1)}, u32[]{:S(2)}, u32[]{:S(2)}) %collective-permute-start.3) | collective-permute-done | bytes 65568 | tf_op jit(solution)/shard_map/ppermute | solution.py:144
  20.7 0.8 %collective-permute-done.4 = f16[2,16,1024]{2,1,0:T(8,128)(2,1)S(1)} collective-permute-done((f16[2,16,1024]{2,1,0:T(8,128)(2,1)S(1)}, f16[2,16,1024]{2,1,0:T(8,128)(2,1)S(1)}, u32[]{:S(2)}, u32[]{:S(2)}) %collective-permute-start.4) | collective-permute-done | bytes 65568 | tf_op jit(solution)/shard_map/ppermute | solution.py:144
  21.5 0.0 collective-permute-done.5
  21.5 0.1 broadcast_select_fusion
  21.6 0.7 %collective-permute-start.7 = (f16[9,2,1024]{2,1,0:T(2,128)(2,1)S(1)}, f16[9,2,1024]{2,1,0:T(2,128)(2,1)S(1)}, u32[]{:S(2)}, u32[]{:S(2)}) collective-permute-start(f16[9,2,1024]{2,1,0:T(2,128)(2,1)S(1)} %get-tuple-element.14), channel_id=1, source_target_pairs={{1,2},{2,1},{5,6},{6,5},{9,10},{10,9},{13,14},{14,13},{17,18},{18,... | collective-permute-start | bytes 110600 | tf_op jit(solution)/shard_map/ppermute | solution.py:198
  22.3 2.9 %collective-permute-start.6 = (f16[9,2,1024]{2,1,0:T(2,128)(2,1)S(1)}, f16[9,2,1024]{2,1,0:T(2,128)(2,1)S(1)}, u32[]{:S(2)}, u32[]{:S(2)}) collective-permute-start(f16[9,2,1024]{2,1,0:T(2,128)(2,1)S(1)} %get-tuple-element.15), channel_id=1, source_target_pairs={{0,1},{1,0},{2,3},{3,2},{4,5},{5,4},{6,7},{7,6},{8,9},{9,8},{10,11... | collective-permute-start | bytes 110600 | tf_op jit(solution)/shard_map/ppermute | solution.py:197
  25.3 0.0 collective-permute-done.7
  25.3 0.8 %collective-permute-done.6 = f16[9,2,1024]{2,1,0:T(2,128)(2,1)S(1)} collective-permute-done((f16[9,2,1024]{2,1,0:T(2,128)(2,1)S(1)}, f16[9,2,1024]{2,1,0:T(2,128)(2,1)S(1)}, u32[]{:S(2)}, u32[]{:S(2)}) %collective-permute-start.6) | collective-permute-done | bytes 36896 | tf_op jit(solution)/shard_map/ppermute | solution.py:197
  26.1 2.5 %shard_map.37 = f32[8,16,1024]{2,1,0:T(8,128)} custom-call(s32[4]{0:T(128)S(1)} %pad_add_fusion.place_ref, f32[2,16,1024]{2,1,0:T(8,128)S(1)} %get-tuple-element.7.refs_0_, f32[2,16,1024]{2,1,0:T(8,128)S(1)} %convert_multiply_fusion.2.refs_1_, f32[2,16,1024]{2,1,0:T(8,128)S(1)} %convert_multiply_fusion.1.refs_2_, ...), custom_call_target="tpu_custom_call" | custom-call | flops 17039360 | bytes 1048576 | tf_op jit(solution)/shard_map/pallas_call | solution.py:126
  (15 shorter events, 0.3 us)
Async XLA Ops:
  0.0 6.8 %copy-start.1 = (s32[4]{0:T(128)S(1)}, s32[4]{0:T(128)}, u32[]{:S(2)}) copy-start(s32[4]{0:T(128)} %param.4) | copy-start | bytes 52
  1.1 8.9 %copy-start = (bf16[1,2,16,1024]{3,2,1,0:T(8,128)(2,1)S(1)}, bf16[1,2,16,1024]{3,2,1,0:T(8,128)(2,1)}, u32[]{:S(2)}) copy-start(bf16[1,2,16,1024]{3,2,1,0:T(8,128)(2,1)} %param.5) | copy-start | bytes 196612
  1.1 9.0 %collective-permute-start.2 = (f16[2,16,1024]{2,1,0:T(8,128)(2,1)S(1)}, f16[2,16,1024]{2,1,0:T(8,128)(2,1)S(1)}, u32[]{:S(2)}, u32[]{:S(2)}) collective-permute-start(f16[2,16,1024]{2,1,0:T(8,128)(2,1)S(1)} %get-tuple-element.9), channel_id=1, source_target_pairs={{0,4},{4,0},{8,12},{12,8},{1,5},{5,1},{9,13},{13,9},{2,6},{6,2},{1... | collective-permute-start | bytes 196616 | tf_op jit(solution)/shard_map/ppermute | solution.py:144
  4.2 7.3 %collective-permute-start.1 = (f16[2,16,1024]{2,1,0:T(8,128)(2,1)S(1)}, f16[2,16,1024]{2,1,0:T(8,128)(2,1)S(1)}, u32[]{:S(2)}, u32[]{:S(2)}) collective-permute-start(f16[2,16,1024]{2,1,0:T(8,128)(2,1)S(1)} %get-tuple-element.10), channel_id=1, source_target_pairs={{0,8},{4,12},{8,0},{12,4},{1,9},{5,13},{9,1},{13,5},{2,10},{6,14},... | collective-permute-start | bytes 196616 | tf_op jit(solution)/shard_map/ppermute | solution.py:144
  6.8 6.1 %collective-permute-start = (f16[2,16,1024]{2,1,0:T(8,128)(2,1)S(1)}, f16[2,16,1024]{2,1,0:T(8,128)(2,1)S(1)}, u32[]{:S(2)}, u32[]{:S(2)}) collective-permute-start(f16[2,16,1024]{2,1,0:T(8,128)(2,1)S(1)} %get-tuple-element.11), channel_id=1, source_target_pairs={{0,12},{4,8},{8,4},{12,0},{1,13},{5,9},{9,5},{13,1},{2,14},{6,10},... | collective-permute-start | bytes 196616 | tf_op jit(solution)/shard_map/ppermute | solution.py:144
  13.8 7.7 %collective-permute-start.5 = (f16[2,16,1024]{2,1,0:T(8,128)(2,1)S(1)}, f16[2,16,1024]{2,1,0:T(8,128)(2,1)S(1)}, u32[]{:S(2)}, u32[]{:S(2)}) collective-permute-start(f16[2,16,1024]{2,1,0:T(8,128)(2,1)S(1)} %get-tuple-element.5), channel_id=1, source_target_pairs={{0,12},{4,8},{8,4},{12,0},{1,13},{5,9},{9,5},{13,1},{2,14},{6,10},... | collective-permute-start | bytes 196616 | tf_op jit(solution)/shard_map/ppermute | solution.py:144
  15.7 5.0 %collective-permute-start.3 = (f16[2,16,1024]{2,1,0:T(8,128)(2,1)S(1)}, f16[2,16,1024]{2,1,0:T(8,128)(2,1)S(1)}, u32[]{:S(2)}, u32[]{:S(2)}) collective-permute-start(f16[2,16,1024]{2,1,0:T(8,128)(2,1)S(1)} %get-tuple-element.13), channel_id=1, source_target_pairs={{0,4},{4,0},{8,12},{12,8},{1,5},{5,1},{9,13},{13,9},{2,6},{6,2},{1... | collective-permute-start | bytes 196616 | tf_op jit(solution)/shard_map/ppermute | solution.py:144
  16.2 5.2 %collective-permute-start.4 = (f16[2,16,1024]{2,1,0:T(8,128)(2,1)S(1)}, f16[2,16,1024]{2,1,0:T(8,128)(2,1)S(1)}, u32[]{:S(2)}, u32[]{:S(2)}) collective-permute-start(f16[2,16,1024]{2,1,0:T(8,128)(2,1)S(1)} %get-tuple-element.12), channel_id=1, source_target_pairs={{0,8},{4,12},{8,0},{12,4},{1,9},{5,13},{9,1},{13,5},{2,10},{6,14},... | collective-permute-start | bytes 196616 | tf_op jit(solution)/shard_map/ppermute | solution.py:144
  21.6 3.7 %collective-permute-start.7 = (f16[9,2,1024]{2,1,0:T(2,128)(2,1)S(1)}, f16[9,2,1024]{2,1,0:T(2,128)(2,1)S(1)}, u32[]{:S(2)}, u32[]{:S(2)}) collective-permute-start(f16[9,2,1024]{2,1,0:T(2,128)(2,1)S(1)} %get-tuple-element.14), channel_id=1, source_target_pairs={{1,2},{2,1},{5,6},{6,5},{9,10},{10,9},{13,14},{14,13},{17,18},{18,... | collective-permute-start | bytes 110600 | tf_op jit(solution)/shard_map/ppermute | solution.py:198
  22.3 3.8 %collective-permute-start.6 = (f16[9,2,1024]{2,1,0:T(2,128)(2,1)S(1)}, f16[9,2,1024]{2,1,0:T(2,128)(2,1)S(1)}, u32[]{:S(2)}, u32[]{:S(2)}) collective-permute-start(f16[9,2,1024]{2,1,0:T(2,128)(2,1)S(1)} %get-tuple-element.15), channel_id=1, source_target_pairs={{0,1},{1,0},{2,3},{3,2},{4,5},{5,4},{6,7},{7,6},{8,9},{9,8},{10,11... | collective-permute-start | bytes 110600 | tf_op jit(solution)/shard_map/ppermute | solution.py:197

commit v2 on v1

v2 whole, which is shorter than its diff:
```python
import functools

import jax
import jax.numpy as jnp
from jax import lax
from jax.experimental import pallas as pl
from jax.experimental.pallas import tpu as pltpu
from jax.sharding import PartitionSpec as P

SCALE = 8192.0
WIRE = jnp.float16
DEPTHS = (0.8, 0.5)
SECOND = (1.0, 1.6)


def pack(values):
    return (values.astype(jnp.float32) * SCALE).astype(WIRE)


def unpack(values):
    return values.astype(jnp.float32) * (1.0 / SCALE)


def lane_roll(a, shift):
    return pltpu.roll(a, shift % a.shape[-1], a.ndim - 1)


def row_roll(a, shift):
    return pltpu.roll(a, shift % a.shape[-2], a.ndim - 2)


def advance(fields):
    around = [
        (lane_roll(f, -1), lane_roll(f, 1), row_roll(f, -1), row_roll(f, 1))
        for f in fields
    ]
    out = []
    hx = [around[l * 4 + 2][0] - around[l * 4 + 2][1] for l in range(2)]
    hy = [around[l * 4 + 2][2] - around[l * 4 + 2][3] for l in range(2)]
    for l in range(2):
        u, v, h, q = fields[l * 4 : l * 4 + 4]
        eu, wu, nu, su = around[l * 4]
        ev, wv, nv, sv = around[l * 4 + 1]
        eh, wh, nh, sh = around[l * 4 + 2]
        eq, wq, nq, sq = around[l * 4 + 3]
        px = hx[0] + SECOND[l] * hx[1]
        py = hy[0] + SECOND[l] * hy[1]
        out.append(0.55 * u + 0.3 * v - 0.125 * px + 0.1 * (eu + wu + nu + su))
        out.append(0.55 * v - 0.3 * u - 0.125 * py + 0.1 * (ev + wv + nv + sv))
        out.append(
            0.6 * h
            - (0.5 * DEPTHS[l]) * ((eu - wu) + (nv - sv))
            + 0.1 * (eh + wh + nh + sh)
        )
        out.append(
            0.6 * q
            - 0.125 * (u * (eq - wq) + v * (nq - sq))
            + 0.1 * (eq + wq + nq + sq)
        )
    return out


def smooth(n):
    around = lane_roll(n, -1) + lane_roll(n, 1) + row_roll(n, -1) + row_roll(n, 1)
    return 0.06 * (4.0 * n + around)


def inner_kernel(parts, *refs):
    piece_refs, (noise_ref, out_ref, raw_ref, once_ref, fog_ref, held) = (
        refs[:parts],
        refs[parts:],
    )
    me = lax.axis_index("particle") if parts > 1 else 0
    total, rows, cols = held.shape
    width = total // parts
    for m in range(parts):
        held[pl.ds((me ^ m) * width, width)] = piece_refs[m][...]
    fields = [held[f] for f in range(total)]
    first = advance(fields)
    for f in range(total):
        raw_ref[f, 2:4] = fields[f][:2]
        raw_ref[f, 4:6] = fields[f][rows - 2 :]
        once_ref[f, 2:4] = first[f][1:3]
        once_ref[f, 4:6] = first[f][rows - 3 : rows - 1]
    second = advance(first)
    for f in range(total):
        if f % 4 == 2:
            n = noise_ref[f // 4].astype(jnp.float32)
            fog_ref[f // 4, 1:4] = n[:3]
            fog_ref[f // 4, 4:7] = n[rows - 3 :]
            out_ref[f] = second[f] + smooth(n)
        else:
            out_ref[f] = second[f]


def ends_kernel(
    parts, inner_ref, raw_ref, once_ref, fog_ref, pair_ref, other_ref, out_hbm, out, sems
):
    me = lax.axis_index("particle") if parts > 1 else 0
    where = lax.axis_index("space")
    even = lax.rem(where, 2) == 0
    no_below, no_above = where == 0, where == lax.axis_size("space") - 1
    total, rows, cols = inner_ref.shape
    width = total // parts
    scale = 1.0 / SCALE

    def received(index):
        pair, other = pair_ref[index] * scale, other_ref[index] * scale
        return (
            jnp.where(no_below, 0.0, jnp.where(even, other, pair)),
            jnp.where(no_above, 0.0, jnp.where(even, pair, other)),
        )

    index = lax.broadcasted_iota(jnp.int32, (8, cols), 0)
    raw = []
    for f in range(total):
        below, above = received(((f // width) ^ me) * width + f % width)
        raw.append(jnp.concatenate([below, raw_ref[f, 2:6], above], axis=0))
    moved = advance(raw)
    once = [
        jnp.where(
            index < 2,
            row_roll(moved[f], -1),
            jnp.where(index > 5, row_roll(moved[f], 1), once_ref[f]),
        )
        for f in range(total)
    ]
    outside = (no_below & (index == 0)) | (no_above & (index == 7))
    once = [jnp.where(outside, 0.0, o) for o in once]
    twice = advance(once)
    fog_below, fog_above = received(total)
    sends = []
    for f in range(total):
        ends = twice[f]
        if f % 4 == 2:
            l = f // 4
            fog = jnp.concatenate(
                [fog_below[l : l + 1], fog_ref[l, 1:7], fog_above[l : l + 1]], axis=0
            )
            ends = ends + smooth(fog)
        out[f, :8] = jnp.where(index < 2, row_roll(ends, -1), inner_ref[f, :8])
        if rows > 16:
            out[f, 8 : rows - 8] = inner_ref[f, 8 : rows - 8]
        out[f, rows - 8 :] = jnp.where(
            index > 5, row_roll(ends, 1), inner_ref[f, rows - 8 :]
        )
        send = pltpu.make_async_copy(out.at[f], out_hbm.at[f], sems.at[f])
        send.start()
        sends.append(send)
    for send in sends:
        send.wait()


VMEM = pl.BlockSpec(memory_space=pltpu.VMEM)
PARAMS = pltpu.CompilerParams(vmem_limit_bytes=32 * 1024 * 1024)


def inner(pieces, noise):
    parts = len(pieces)
    total = parts * pieces[0].shape[0]
    rows, cols = pieces[0].shape[1:]
    shapes = [(total, rows, cols), (total, 8, cols), (total, 8, cols), (2, 8, cols)]
    return pl.pallas_call(
        functools.partial(inner_kernel, parts),
        out_shape=[jax.ShapeDtypeStruct(shape, jnp.float32) for shape in shapes],
        in_specs=[VMEM] * (parts + 1),
        out_specs=[VMEM] * 4,
        scratch_shapes=[pltpu.VMEM(shapes[0], jnp.float32)],
        compiler_params=PARAMS,
        cost_estimate=pl.CostEstimate(
            flops=110 * total * rows * cols, bytes_accessed=1 << 20, transcendentals=0
        ),
    )(*pieces, noise)


def ends(parts, kept, pair, other):
    total, rows, cols = kept[0].shape
    return pl.pallas_call(
        functools.partial(ends_kernel, parts),
        out_shape=jax.ShapeDtypeStruct((total, rows, cols), jnp.float32),
        in_specs=[VMEM] * 6,
        out_specs=pl.BlockSpec(memory_space=pl.ANY),
        scratch_shapes=[
            pltpu.VMEM((total, rows, cols), jnp.float32),
            pltpu.SemaphoreType.DMA((total,)),
        ],
        compiler_params=PARAMS,
        cost_estimate=pl.CostEstimate(
            flops=110 * total * 8 * cols, bytes_accessed=1 << 20, transcendentals=0
        ),
    )(*kept, pair, other)


def fetch_by_permutes(state, ancestors, count, me):
    def swap(a, m):
        return lax.ppermute(a, "particle", [(i, i ^ m) for i in range(count)])

    fields, rows, cols = state.shape
    cut = state.reshape(count, fields // count, rows, cols)

    def part(m):
        return pack(lax.dynamic_index_in_dim(cut, me ^ m, 0, keepdims=False))

    own, *sent = lax.optimization_barrier([part(m) for m in range(count)])
    here = [own] + [swap(sent[m - 1], m) for m in range(1, count)]

    code = jnp.sum((ancestors ^ me) << (4 * jnp.arange(count, dtype=jnp.int32)))

    def pick(slot):
        which = (code >> (4 * slot)) & (count - 1)
        chosen = here[0]
        for m in range(1, count):
            chosen = jnp.where(which == m, here[m], chosen)
        return chosen

    own, *sent = lax.optimization_barrier([pick(me ^ m) for m in range(count)])
    return [own] + [swap(sent[m - 1], m) for m in range(1, count)]


def fetch_by_all_to_all(state, ancestors, count):
    fields, rows, cols = state.shape
    cut = pack(state).reshape(fields, rows, count, cols // count).transpose(2, 0, 1, 3)
    here = lax.all_to_all(cut, "particle", split_axis=0, concat_axis=0, tiled=True)
    chosen = jnp.take(here, ancestors, axis=0)
    back = lax.all_to_all(chosen, "particle", split_axis=0, concat_axis=0, tiled=True)
    return back.transpose(1, 2, 0, 3).reshape(fields, rows, cols)


def per_device(state, ancestors, noise):
    state, noise = state[0], noise[0]
    count = lax.axis_size("particle")
    me = lax.axis_index("particle")
    if count in (2, 4, 8):
        pieces = fetch_by_permutes(state, ancestors, count, me)
    else:
        pieces = [fetch_by_all_to_all(state, ancestors, count)]

    blocks = lax.axis_size("space")
    where = lax.axis_index("space")
    even = where % 2 == 0
    low = jnp.concatenate(
        [p[:, :2] for p in pieces] + [pack(noise[:, :1]).reshape(1, 2, -1)], axis=0
    )
    high = jnp.concatenate(
        [p[:, -2:] for p in pieces] + [pack(noise[:, -1:]).reshape(1, 2, -1)], axis=0
    )
    pairs = [(i, i ^ 1) for i in range(blocks)]
    others = [(i, (i + 1 if i % 2 else i - 1) % blocks) for i in range(blocks)]
    pair = lax.ppermute(jnp.where(even, high, low), "space", pairs)
    other = lax.ppermute(jnp.where(even, low, high), "space", others)

    kept = inner([unpack(p) for p in pieces], noise)
    out = ends(
        len(pieces), kept, pair.astype(jnp.float32), other.astype(jnp.float32)
    )
    return out[None]


def solution(mesh):
    in_specs = (
        P(("run", "particle"), None, "space", None),
        P("run"),
        P(("run", "particle"), None, "space", None),
    )
    out_specs = P(("run", "particle"), None, "space", None)
    return jax.shard_map(
        per_device, mesh=mesh, in_specs=in_specs, out_specs=out_specs, check_vma=False
    )
```

time: 29.1 us -> 27 us (0.928); the launches traced: 28.6 us -> 26.9 us
  starting transfers between devices: 13.8 us -> 11.9 us
  waiting for transfers between devices: 6.37 us -> 7.62 us
  local copies, waits for them, and re-layouts: 0.79 us -> 0.2 us
  other arithmetic: 2.43 us -> 2.1 us
    ppermute x1, starting transfers between devices: 2.92 us -> 1.59 us  [per_device(): pair = lax.ppermute(jnp.where(even, high, low), 'space', pairs)]
    ppermute x1, waiting for transfers between devices: 0.01 us -> 1.14 us  [per_device(): other = lax.ppermute(jnp.where(even, low, high), 'space', others)]
    select_n x2 -> x1, other arithmetic: 1.01 us -> 0.1 us  [pick(): chosen = jnp.where(which == m, here[m], chosen)]
    ppermute x6, waiting for transfers between devices: 5.61 us -> 6.48 us  [swap(): return lax.ppermute(a, 'particle', [(i, i ^ m) for i in range(count)])]
    ppermute x1, waiting for transfers between devices: 0.76 us -> 0.01 us  [per_device(): pair = lax.ppermute(jnp.where(even, high, low), 'space', pairs)]
    dynamic_slice x1 -> x0, local copies, waits for them, and re-layouts: 0.65 us -> none  [pick(): which = lax.dynamic_index_in_dim(ancestors, slot, 0, keepdims=False) ^ me]
    reduce_sum x0 -> x1, other arithmetic: none -> 0.63 us  [fetch_by_permutes(): code = jnp.sum((ancestors ^ me) << 4 * jnp.arange(count, dtype=jnp.int32))]
    ppermute x1, starting transfers between devices: 0.66 us -> 0.07 us  [per_device(): other = lax.ppermute(jnp.where(even, low, high), 'space', others)]
  transfers between devices with their start and end apart: 8 -> 8, of which waited for: 5 -> 5; matrix products, arithmetic and copies ran while one was open for 4% -> 3% of each run, Pallas kernels for 0% -> 3%
where the time goes in v2:
time: 27 us; the launch traced here: 26.9 us
  starting transfers between devices  11.9 us (44%)
  waiting for transfers between devices  7.62 us (28%)
  between operations  2.76 us (10%)
  Pallas kernels  2.23 us (8%)
  other arithmetic  2.1 us (8%)
    ppermute x6, starting transfers between devices, swap(): return lax.ppermute(a, 'particle', [(i, i ^ m) for i in range(count)])  10.3 us
    ppermute x6, waiting for transfers between devices, swap(): return lax.ppermute(a, 'particle', [(i, i ^ m) for i in range(count)])  6.48 us
    ppermute x1, starting transfers between devices, per_device(): pair = lax.ppermute(jnp.where(even, high, low), 'space', pairs)  1.59 us
    pallas_call x1, Pallas kernels, ends(): pl.pallas_call(functools.partial(ends_kernel, parts), out_shape=jax.Shape...  1.32 us
    convert_element_type x1, other arithmetic, pack(): return (values.astype(jnp.float32) * SCALE).astype(WIRE)  1.15 us
    ppermute x1, waiting for transfers between devices, per_device(): other = lax.ppermute(jnp.where(even, low, high), 'space', others)  1.14 us
    pallas_call x1, Pallas kernels, inner(): pl.pallas_call(functools.partial(inner_kernel, parts), out_shape=[jax.Sha...  0.92 us
    reduce_sum x1, other arithmetic, fetch_by_permutes(): code = jnp.sum((ancestors ^ me) << 4 * jnp.arange(count, dtype=jnp.int32))  0.63 us
  transfers between devices with their start and end apart: 8, of which 5 were waited for; matrix products, arithmetic and copies ran while one was open for 3% of the time, Pallas kernels for 3%

profile of v2, /device:TPU:0, one launch (start us, length us, event | category | flops | bytes accessed | tf_op | source)
XLA Modules:
  0.0 26.9 jit_solution(829513893042216156)
XLA Ops:
  0.0 1.2 %fusion.3 = (f16[2,16,1024]{2,1,0:T(8,128)(2,1)S(1)}, f16[2,16,1024]{2,1,0:T(8,128)(2,1)S(1)}, f16[2,16,1024]{2,1,0:T(8,128)(2,1)S(1)}, f16[2,16,1024]{2,1,0:T(8,128)(2,1)S(1)}) fusion(f32[4,2,16,1024]{3,2,1,0:T(8,128)} %bitcast.21, s32[]{:T(128)S(6)} %select_n.110, s32[]{:T(128)S(6)} %select_n.109, s32[]{:T(128)S(6)} %select_n.108, s32[]{:T(128)S(6)} %select_n.107), kind=kLoop, calls=%fused_computation.13 | loop fusion | flops 262144 | bytes 786448 | tf_op jit(solution)/shard_map/convert_element_type | solution.py:17
  1.2 0.0 copy-start
  1.2 5.1 %collective-permute-start = (f16[2,16,1024]{2,1,0:T(8,128)(2,1)S(1)}, f16[2,16,1024]{2,1,0:T(8,128)(2,1)S(1)}, u32[]{:S(2)}, u32[]{:S(2)}) collective-permute-start(f16[2,16,1024]{2,1,0:T(8,128)(2,1)S(1)} %get-tuple-element.17), channel_id=1, source_target_pairs={{0,12},{4,8},{8,4},{12,0},{1,13},{5,9},{9,5},{13,1},{2,14},{6,10},... | collective-permute-start | bytes 196616 | tf_op jit(solution)/shard_map/ppermute | solution.py:196
  6.3 0.0 collective-permute-start.1
  6.3 0.6 %collective-permute-start.2 = (f16[2,16,1024]{2,1,0:T(8,128)(2,1)S(1)}, f16[2,16,1024]{2,1,0:T(8,128)(2,1)S(1)}, u32[]{:S(2)}, u32[]{:S(2)}) collective-permute-start(f16[2,16,1024]{2,1,0:T(8,128)(2,1)S(1)} %get-tuple-element.19), channel_id=1, source_target_pairs={{0,4},{4,0},{8,12},{12,8},{1,5},{5,1},{9,13},{13,9},{2,6},{6,2},{1... | collective-permute-start | bytes 196616 | tf_op jit(solution)/shard_map/ppermute | solution.py:196
  6.9 0.6 %shift-left_reduce_fusion = s32[]{:T(128)} fusion(s32[4]{0:T(128)S(1)} %copy-done.1, s32[]{:T(128)S(6)} %axis_index.23), kind=kLoop, calls=%fused_computation.33 | loop fusion | flops 15 | bytes 24 | tf_op jit(solution)/shard_map/reduce_sum | solution.py:207
  10.2 0.1 copy.7
  10.3 0.0 collective-permute-done
  10.3 1.6 %collective-permute-done.1 = f16[2,16,1024]{2,1,0:T(8,128)(2,1)S(1)} collective-permute-done((f16[2,16,1024]{2,1,0:T(8,128)(2,1)S(1)}, f16[2,16,1024]{2,1,0:T(8,128)(2,1)S(1)}, u32[]{:S(2)}, u32[]{:S(2)}) %collective-permute-start.1) | collective-permute-done | bytes 65568 | tf_op jit(solution)/shard_map/ppermute | solution.py:196
  11.9 0.0 collective-permute-done.2
  11.9 0.1 select_select_fusion
  12.0 1.1 %collective-permute-start.3 = (f16[2,16,1024]{2,1,0:T(8,128)(2,1)S(1)}, f16[2,16,1024]{2,1,0:T(8,128)(2,1)S(1)}, u32[]{:S(2)}, u32[]{:S(2)}) collective-permute-start(f16[2,16,1024]{2,1,0:T(8,128)(2,1)S(1)} %get-tuple-element.22), channel_id=1, source_target_pairs={{0,4},{4,0},{8,12},{12,8},{1,5},{5,1},{9,13},{13,9},{2,6},{6,2},{1... | collective-permute-start | bytes 196616 | tf_op jit(solution)/shard_map/ppermute | solution.py:196
  13.2 2.3 %collective-permute-start.4 = (f16[2,16,1024]{2,1,0:T(8,128)(2,1)S(1)}, f16[2,16,1024]{2,1,0:T(8,128)(2,1)S(1)}, u32[]{:S(2)}, u32[]{:S(2)}) collective-permute-start(f16[2,16,1024]{2,1,0:T(8,128)(2,1)S(1)} %get-tuple-element.23), channel_id=1, source_target_pairs={{0,8},{4,12},{8,0},{12,4},{1,9},{5,13},{9,1},{13,5},{2,10},{6,14},... | collective-permute-start | bytes 196616 | tf_op jit(solution)/shard_map/ppermute | solution.py:196
  15.5 1.1 %collective-permute-start.5 = (f16[2,16,1024]{2,1,0:T(8,128)(2,1)S(1)}, f16[2,16,1024]{2,1,0:T(8,128)(2,1)S(1)}, u32[]{:S(2)}, u32[]{:S(2)}) collective-permute-start(f16[2,16,1024]{2,1,0:T(8,128)(2,1)S(1)} %get-tuple-element.24), channel_id=1, source_target_pairs={{0,12},{4,8},{8,4},{12,0},{1,13},{5,9},{9,5},{13,1},{2,14},{6,10},... | collective-permute-start | bytes 196616 | tf_op jit(solution)/shard_map/ppermute | solution.py:196
  16.6 0.2 collective-permute-done.3
  16.8 3.1 %collective-permute-done.4 = f16[2,16,1024]{2,1,0:T(8,128)(2,1)S(1)} collective-permute-done((f16[2,16,1024]{2,1,0:T(8,128)(2,1)S(1)}, f16[2,16,1024]{2,1,0:T(8,128)(2,1)S(1)}, u32[]{:S(2)}, u32[]{:S(2)}) %collective-permute-start.4) | collective-permute-done | bytes 65568 | tf_op jit(solution)/shard_map/ppermute | solution.py:196
  19.9 1.6 %collective-permute-done.5 = f16[2,16,1024]{2,1,0:T(8,128)(2,1)S(1)} collective-permute-done((f16[2,16,1024]{2,1,0:T(8,128)(2,1)S(1)}, f16[2,16,1024]{2,1,0:T(8,128)(2,1)S(1)}, u32[]{:S(2)}, u32[]{:S(2)}) %collective-permute-start.5) | collective-permute-done | bytes 65568 | tf_op jit(solution)/shard_map/ppermute | solution.py:196
  21.6 0.1 broadcast_select_fusion
  21.7 0.1 collective-permute-start.7
  21.7 1.6 %collective-permute-start.6 = (f16[9,2,1024]{2,1,0:T(2,128)(2,1)S(1)}, f16[9,2,1024]{2,1,0:T(2,128)(2,1)S(1)}, u32[]{:S(2)}, u32[]{:S(2)}) collective-permute-start(f16[9,2,1024]{2,1,0:T(2,128)(2,1)S(1)} %get-tuple-element.38), channel_id=1, source_target_pairs={{0,1},{1,0},{2,3},{3,2},{4,5},{5,4},{6,7},{7,6},{8,9},{9,8},{10,11... | collective-permute-start | bytes 110600 | tf_op jit(solution)/shard_map/ppermute | solution.py:249
  23.4 0.9 %shard_map.37 = (f32[8,16,1024]{2,1,0:T(8,128)S(1)}, f32[8,8,1024]{2,1,0:T(8,128)S(1)}, f32[8,8,1024]{2,1,0:T(8,128)S(1)}, f32[2,8,1024]{2,1,0:T(8,128)S(1)}) custom-call(f32[2,16,1024]{2,1,0:T(8,128)S(1)} %convert_multiply_fusion.3.refs_0_, f32[2,16,1024]{2,1,0:T(8,128)S(1)} %convert_multiply_fusion.2.refs_1_, ...), custom_call_target="tpu_custom_call" | custom-call | flops 14417920 | bytes 1048576 | tf_op jit(solution)/shard_map/pallas_call | solution.py:163
  24.3 1.1 %collective-permute-done.7 = f16[9,2,1024]{2,1,0:T(2,128)(2,1)S(1)} collective-permute-done((f16[9,2,1024]{2,1,0:T(2,128)(2,1)S(1)}, f16[9,2,1024]{2,1,0:T(2,128)(2,1)S(1)}, u32[]{:S(2)}, u32[]{:S(2)}) %collective-permute-start.7) | collective-permute-done | bytes 36896 | tf_op jit(solution)/shard_map/ppermute | solution.py:250
  25.5 0.0 collective-permute-done.6
  25.5 1.3 %shard_map.38 = f32[8,16,1024]{2,1,0:T(8,128)} custom-call(f32[8,16,1024]{2,1,0:T(8,128)S(1)} %get-tuple-element.25.inner_ref, f32[8,8,1024]{2,1,0:T(8,128)S(1)} %get-tuple-element.26.raw_ref, f32[8,8,1024]{2,1,0:T(8,128)S(1)} %get-tuple-element.27.once_ref, f32[2,8,1024]{2,1,0:T(8,128)S(1)} %get-tuple-element.28.fog_ref, ...), custom_call_target="tpu_custom_call" | custom-call | flops 7208960 | bytes 1048576 | tf_op jit(solution)/shard_map/pallas_call | solution.py:178
  (15 shorter events, 0.3 us)
Async XLA Ops:
  0.0 6.9 %copy-start.1 = (s32[4]{0:T(128)S(1)}, s32[4]{0:T(128)}, u32[]{:S(2)}) copy-start(s32[4]{0:T(128)} %param.4) | copy-start | bytes 52
  1.2 9.0 %copy-start = (bf16[1,2,16,1024]{3,2,1,0:T(8,128)(2,1)S(1)}, bf16[1,2,16,1024]{3,2,1,0:T(8,128)(2,1)}, u32[]{:S(2)}) copy-start(bf16[1,2,16,1024]{3,2,1,0:T(8,128)(2,1)} %param.5) | copy-start | bytes 196612
  1.2 9.1 %collective-permute-start = (f16[2,16,1024]{2,1,0:T(8,128)(2,1)S(1)}, f16[2,16,1024]{2,1,0:T(8,128)(2,1)S(1)}, u32[]{:S(2)}, u32[]{:S(2)}) collective-permute-start(f16[2,16,1024]{2,1,0:T(8,128)(2,1)S(1)} %get-tuple-element.17), channel_id=1, source_target_pairs={{0,12},{4,8},{8,4},{12,0},{1,13},{5,9},{9,5},{13,1},{2,14},{6,10},... | collective-permute-start | bytes 196616 | tf_op jit(solution)/shard_map/ppermute | solution.py:196
  6.3 5.6 %collective-permute-start.1 = (f16[2,16,1024]{2,1,0:T(8,128)(2,1)S(1)}, f16[2,16,1024]{2,1,0:T(8,128)(2,1)S(1)}, u32[]{:S(2)}, u32[]{:S(2)}) collective-permute-start(f16[2,16,1024]{2,1,0:T(8,128)(2,1)S(1)} %get-tuple-element.18), channel_id=1, source_target_pairs={{0,8},{4,12},{8,0},{12,4},{1,9},{5,13},{9,1},{13,5},{2,10},{6,14},... | collective-permute-start | bytes 196616 | tf_op jit(solution)/shard_map/ppermute | solution.py:196
  6.3 5.6 %collective-permute-start.2 = (f16[2,16,1024]{2,1,0:T(8,128)(2,1)S(1)}, f16[2,16,1024]{2,1,0:T(8,128)(2,1)S(1)}, u32[]{:S(2)}, u32[]{:S(2)}) collective-permute-start(f16[2,16,1024]{2,1,0:T(8,128)(2,1)S(1)} %get-tuple-element.19), channel_id=1, source_target_pairs={{0,4},{4,0},{8,12},{12,8},{1,5},{5,1},{9,13},{13,9},{2,6},{6,2},{1... | collective-permute-start | bytes 196616 | tf_op jit(solution)/shard_map/ppermute | solution.py:196
  12.0 4.7 %collective-permute-start.3 = (f16[2,16,1024]{2,1,0:T(8,128)(2,1)S(1)}, f16[2,16,1024]{2,1,0:T(8,128)(2,1)S(1)}, u32[]{:S(2)}, u32[]{:S(2)}) collective-permute-start(f16[2,16,1024]{2,1,0:T(8,128)(2,1)S(1)} %get-tuple-element.22), channel_id=1, source_target_pairs={{0,4},{4,0},{8,12},{12,8},{1,5},{5,1},{9,13},{13,9},{2,6},{6,2},{1... | collective-permute-start | bytes 196616 | tf_op jit(solution)/shard_map/ppermute | solution.py:196
  13.2 6.7 %collective-permute-start.4 = (f16[2,16,1024]{2,1,0:T(8,128)(2,1)S(1)}, f16[2,16,1024]{2,1,0:T(8,128)(2,1)S(1)}, u32[]{:S(2)}, u32[]{:S(2)}) collective-permute-start(f16[2,16,1024]{2,1,0:T(8,128)(2,1)S(1)} %get-tuple-element.23), channel_id=1, source_target_pairs={{0,8},{4,12},{8,0},{12,4},{1,9},{5,13},{9,1},{13,5},{2,10},{6,14},... | collective-permute-start | bytes 196616 | tf_op jit(solution)/shard_map/ppermute | solution.py:196
  15.5 6.1 %collective-permute-start.5 = (f16[2,16,1024]{2,1,0:T(8,128)(2,1)S(1)}, f16[2,16,1024]{2,1,0:T(8,128)(2,1)S(1)}, u32[]{:S(2)}, u32[]{:S(2)}) collective-permute-start(f16[2,16,1024]{2,1,0:T(8,128)(2,1)S(1)} %get-tuple-element.24), channel_id=1, source_target_pairs={{0,12},{4,8},{8,4},{12,0},{1,13},{5,9},{9,5},{13,1},{2,14},{6,10},... | collective-permute-start | bytes 196616 | tf_op jit(solution)/shard_map/ppermute | solution.py:196
  21.7 3.8 %collective-permute-start.7 = (f16[9,2,1024]{2,1,0:T(2,128)(2,1)S(1)}, f16[9,2,1024]{2,1,0:T(2,128)(2,1)S(1)}, u32[]{:S(2)}, u32[]{:S(2)}) collective-permute-start(f16[9,2,1024]{2,1,0:T(2,128)(2,1)S(1)} %get-tuple-element.37), channel_id=1, source_target_pairs={{0,3},{1,2},{2,1},{3,0},{4,7},{5,6},{6,5},{7,4},{8,11},{9,10},{10,... | collective-permute-start | bytes 110600 | tf_op jit(solution)/shard_map/ppermute | solution.py:250
  21.7 3.7 %collective-permute-start.6 = (f16[9,2,1024]{2,1,0:T(2,128)(2,1)S(1)}, f16[9,2,1024]{2,1,0:T(2,128)(2,1)S(1)}, u32[]{:S(2)}, u32[]{:S(2)}) collective-permute-start(f16[9,2,1024]{2,1,0:T(2,128)(2,1)S(1)} %get-tuple-element.38), channel_id=1, source_target_pairs={{0,1},{1,0},{2,3},{3,2},{4,5},{5,4},{6,7},{7,6},{8,9},{9,8},{10,11... | collective-permute-start | bytes 110600 | tf_op jit(solution)/shard_map/ppermute | solution.py:249

commit v3 on v2

--- a/solution.py
+++ b/solution.py
@@ -2,6 +2,7 @@
 
 import jax
 import jax.numpy as jnp
+import numpy as np
 from jax import lax
 from jax.experimental import pallas as pl
 from jax.experimental.pallas import tpu as pltpu
@@ -11,6 +12,10 @@
 WIRE = jnp.float16
 DEPTHS = (0.8, 0.5)
 SECOND = (1.0, 1.6)
+
+
+ACROSS = 3
+CHUNKS = 2
 
 
 def pack(values):
@@ -66,16 +71,12 @@
 
 
 def inner_kernel(parts, *refs):
-    piece_refs, (noise_ref, out_ref, raw_ref, once_ref, fog_ref, held) = (
+    piece_refs, (noise_ref, out_ref, raw_ref, once_ref, fog_ref) = (
         refs[:parts],
         refs[parts:],
     )
-    me = lax.axis_index("particle") if parts > 1 else 0
-    total, rows, cols = held.shape
-    width = total // parts
-    for m in range(parts):
-        held[pl.ds((me ^ m) * width, width)] = piece_refs[m][...]
-    fields = [held[f] for f in range(total)]
+    total, rows, cols = out_ref.shape
+    fields = [ref[i] for ref in piece_refs for i in range(ref.shape[0])]
     first = advance(fields)
     for f in range(total):
         raw_ref[f, 2:4] = fields[f][:2]
@@ -94,14 +95,12 @@
 
 
 def ends_kernel(
-    parts, inner_ref, raw_ref, once_ref, fog_ref, pair_ref, other_ref, out_hbm, out, sems
+    inner_ref, raw_ref, once_ref, fog_ref, pair_ref, other_ref, out_hbm, out, sems
 ):
-    me = lax.axis_index("particle") if parts > 1 else 0
     where = lax.axis_index("space")
     even = lax.rem(where, 2) == 0
     no_below, no_above = where == 0, where == lax.axis_size("space") - 1
     total, rows, cols = inner_ref.shape
-    width = total // parts
     scale = 1.0 / SCALE
 
     def received(index):
@@ -114,7 +113,7 @@
     index = lax.broadcasted_iota(jnp.int32, (8, cols), 0)
     raw = []
     for f in range(total):
-        below, above = received(((f // width) ^ me) * width + f % width)
+        below, above = received(f)
         raw.append(jnp.concatenate([below, raw_ref[f, 2:6], above], axis=0))
     moved = advance(raw)
     once = [
@@ -157,7 +156,7 @@
 
 def inner(pieces, noise):
     parts = len(pieces)
-    total = parts * pieces[0].shape[0]
+    total = sum(p.shape[0] for p in pieces)
     rows, cols = pieces[0].shape[1:]
     shapes = [(total, rows, cols), (total, 8, cols), (total, 8, cols), (2, 8, cols)]
     return pl.pallas_call(
@@ -165,7 +164,6 @@
         out_shape=[jax.ShapeDtypeStruct(shape, jnp.float32) for shape in shapes],
         in_specs=[VMEM] * (parts + 1),
         out_specs=[VMEM] * 4,
-        scratch_shapes=[pltpu.VMEM(shapes[0], jnp.float32)],
         compiler_params=PARAMS,
         cost_estimate=pl.CostEstimate(
             flops=110 * total * rows * cols, bytes_accessed=1 << 20, transcendentals=0
@@ -173,10 +171,10 @@
     )(*pieces, noise)
 
 
-def ends(parts, kept, pair, other):
+def ends(kept, pair, other):
     total, rows, cols = kept[0].shape
     return pl.pallas_call(
-        functools.partial(ends_kernel, parts),
+        ends_kernel,
         out_shape=jax.ShapeDtypeStruct((total, rows, cols), jnp.float32),
         in_specs=[VMEM] * 6,
         out_specs=pl.BlockSpec(memory_space=pl.ANY),
@@ -191,30 +189,37 @@
     )(*kept, pair, other)
 
 
-def fetch_by_permutes(state, ancestors, count, me):
-    def swap(a, m):
-        return lax.ppermute(a, "particle", [(i, i ^ m) for i in range(count)])
-
-    fields, rows, cols = state.shape
-    cut = state.reshape(count, fields // count, rows, cols)
-
-    def part(m):
-        return pack(lax.dynamic_index_in_dim(cut, me ^ m, 0, keepdims=False))
-
-    own, *sent = lax.optimization_barrier([part(m) for m in range(count)])
-    here = [own] + [swap(sent[m - 1], m) for m in range(1, count)]
-
-    code = jnp.sum((ancestors ^ me) << (4 * jnp.arange(count, dtype=jnp.int32)))
-
-    def pick(slot):
-        which = (code >> (4 * slot)) & (count - 1)
-        chosen = here[0]
-        for m in range(1, count):
-            chosen = jnp.where(which == m, here[m], chosen)
-        return chosen
-
-    own, *sent = lax.optimization_barrier([pick(me ^ m) for m in range(count)])
-    return [own] + [swap(sent[m - 1], m) for m in range(1, count)]
+def fetch_by_permutes(state, ancestors, me, even):
+    blocks = lax.axis_size("space")
+
+    def swap(a, even_mask, odd_mask):
+        masks = (even_mask, odd_mask)
+        pairs = [
+            (i * blocks + s, (i ^ masks[s % 2]) * blocks + s)
+            for i in range(4)
+            for s in range(blocks)
+        ]
+        return lax.ppermute(a, ("particle", "space"), pairs)
+
+    size = state.shape[0] // CHUNKS
+    parts = [state[c * size : (c + 1) * size] for c in range(CHUNKS)]
+    owns = lax.optimization_barrier([pack(p) for p in parts])
+    gots = [swap(own, 1, ACROSS) for own in owns]
+    places = 4 * np.arange(4, dtype=np.int32)
+    code = jnp.sum(ancestors << places) ^ (me * np.sum(1 << places).astype(np.int32))
+    first = jnp.where(even, 1, ACROSS)
+    second = jnp.where(even, ACROSS, 1)
+
+    def distance(slot):
+        return (code >> (4 * slot)) & 3
+
+    keep = distance(me ^ second) == 0
+    mine = distance(me)
+    result = []
+    for own, got in zip(owns, gots):
+        last = swap(jnp.where(keep, own, got), ACROSS, 1)
+        result.append(jnp.where(mine == 0, own, jnp.where(mine == first, got, last)))
+    return result
 
 
 def fetch_by_all_to_all(state, ancestors, count):
@@ -230,29 +235,26 @@
     state, noise = state[0], noise[0]
     count = lax.axis_size("particle")
     me = lax.axis_index("particle")
-    if count in (2, 4, 8):
-        pieces = fetch_by_permutes(state, ancestors, count, me)
+    blocks = lax.axis_size("space")
+    even = lax.axis_index("space") & 1 == 0
+    if count == 4:
+        pieces = fetch_by_permutes(state, ancestors, me, even)
     else:
         pieces = [fetch_by_all_to_all(state, ancestors, count)]
 
-    blocks = lax.axis_size("space")
-    where = lax.axis_index("space")
-    even = where % 2 == 0
-    low = jnp.concatenate(
-        [p[:, :2] for p in pieces] + [pack(noise[:, :1]).reshape(1, 2, -1)], axis=0
-    )
-    high = jnp.concatenate(
-        [p[:, -2:] for p in pieces] + [pack(noise[:, -1:]).reshape(1, 2, -1)], axis=0
-    )
+    fog_low = pack(noise[:, :1]).reshape(1, 2, -1)
+    fog_high = pack(noise[:, -1:]).reshape(1, 2, -1)
+    sides = [(p[:, :2], p[:, -2:]) for p in pieces] + [(fog_low, fog_high)]
+    to_pair = jnp.concatenate([jnp.where(even, h, l) for l, h in sides], axis=0)
+    to_other = jnp.concatenate([jnp.where(even, l, h) for l, h in sides], axis=0)
+    to_other, to_pair = lax.optimization_barrier((to_other, to_pair))
     pairs = [(i, i ^ 1) for i in range(blocks)]
     others = [(i, (i + 1 if i % 2 else i - 1) % blocks) for i in range(blocks)]
-    pair = lax.ppermute(jnp.where(even, high, low), "space", pairs)
-    other = lax.ppermute(jnp.where(even, low, high), "space", others)
+    other = lax.ppermute(to_other, "space", others)
+    pair = lax.ppermute(to_pair, "space", pairs)
 
     kept = inner([unpack(p) for p in pieces], noise)
-    out = ends(
-        len(pieces), kept, pair.astype(jnp.float32), other.astype(jnp.float32)
-    )
+    out = ends(kept, pair.astype(jnp.float32), other.astype(jnp.float32))
     return out[None]
 
 

time: 27 us -> 24.9 us (0.922)
  between operations: 2.76 us -> 0.78 us
  local copies, waits for them, and re-layouts: 0.2 us -> 0.74 us
  waiting for transfers between devices: 7.62 us -> 7.1 us
    unnamed x9 -> x5, local copies, waits for them, and re-layouts: 0.18 us -> 0.73 us
    ppermute x8 -> x6, waiting for transfers between devices: 7.62 us -> 7.1 us  [the longest x4 6.2 us: swap(): return lax.ppermute(a, ('particle', 'space'), pairs)]
    ppermute x8 -> x6, starting transfers between devices: 11.9 us -> 11.7 us  [the longest x4 10 us: swap(): return lax.ppermute(a, ('particle', 'space'), pairs)]
  transfers between devices with their start and end apart: 8 -> 6, of which waited for: 5 -> 4; matrix products, arithmetic and copies ran while one was open for 3% -> 4% of each run, Pallas kernels for 3% -> 4%
where the time goes in v3:
time: 24.9 us; the launch traced here: 24.8 us
  starting transfers between devices  11.7 us (47%)
  waiting for transfers between devices  7.1 us (29%)
  other arithmetic  2.25 us (9%)
  Pallas kernels  2.19 us (9%)
  between operations  0.78 us (3%)
  local copies, waits for them, and re-layouts  0.74 us (3%)
    ppermute x4, starting transfers between devices, swap(): return lax.ppermute(a, ('particle', 'space'), pairs)  10 us
    ppermute x4, waiting for transfers between devices, swap(): return lax.ppermute(a, ('particle', 'space'), pairs)  6.2 us
    ppermute x1, starting transfers between devices, per_device(): other = lax.ppermute(to_other, 'space', others)  1.61 us
    pallas_call x1, Pallas kernels, ends(): pl.pallas_call(ends_kernel, out_shape=jax.ShapeDtypeStruct((total, rows,...  1.32 us
    convert_element_type x1, other arithmetic, pack(): return (values.astype(jnp.float32) * SCALE).astype(WIRE)  1.11 us
    ppermute x1, waiting for transfers between devices, per_device(): other = lax.ppermute(to_other, 'space', others)  0.89 us
    pallas_call x1, Pallas kernels, inner(): pl.pallas_call(functools.partial(inner_kernel, parts), out_shape=[jax.Sha...  0.87 us
    unnamed x5, local copies, waits for them, and re-layouts  0.73 us
  transfers between devices with their start and end apart: 6, of which 4 were waited for; matrix products, arithmetic and copies ran while one was open for 4% of the time, Pallas kernels for 4%

profile of v3, /device:TPU:0, one launch (start us, length us, event | category | flops | bytes accessed | tf_op | source)
XLA Modules:
  0.0 24.8 jit_solution(8260824063581796475)
XLA Ops:
  0.0 0.0 copy-start
  0.0 1.1 %fusion.1 = (f16[4,16,1024]{2,1,0:T(8,128)(2,1)S(1)}, f16[4,16,1024]{2,1,0:T(8,128)(2,1)S(1)}) fusion(f32[1,8,16,1024]{3,2,1,0:T(8,128)} %param.4), kind=kLoop, calls=%fused_computation.5 | loop fusion | flops 262144 | bytes 786432 | tf_op jit(solution)/shard_map/convert_element_type | solution.py:22
  1.1 3.1 %collective-permute-start = (f16[4,16,1024]{2,1,0:T(8,128)(2,1)S(1)}, f16[4,16,1024]{2,1,0:T(8,128)(2,1)S(1)}, u32[]{:S(2)}, u32[]{:S(2)}) collective-permute-start(f16[4,16,1024]{2,1,0:T(8,128)(2,1)S(1)} %get-tuple-element.13), channel_id=1, source_target_pairs={{0,4},{1,13},{2,6},{3,15},{4,0},{5,9},{6,2},{7,11},{8,12},{9,5},{1... | collective-permute-start | bytes 393224 | tf_op jit(solution)/shard_map/ppermute | solution.py:202
  4.2 0.1 collective-permute-start.2
  4.3 0.0 copy-start.1
  4.3 0.7 %copy-done.1 = s32[4]{0:T(128)S(1)} copy-done((s32[4]{0:T(128)S(1)}, s32[4]{0:T(128)}, u32[]{:S(2)}) %copy-start.1) | copy-done | bytes 40
  4.9 0.6 %shift-left_reduce_fusion = s32[]{:T(128)} fusion(s32[4]{0:T(128)S(1)} %copy-done.1), kind=kLoop, calls=%fused_computation.23 | loop fusion | flops 11 | bytes 20 | tf_op jit(solution)/shard_map/reduce_sum | solution.py:209
  6.2 0.0 copy-done
  6.3 0.1 copy.8
  6.4 2.2 %collective-permute-done = f16[4,16,1024]{2,1,0:T(8,128)(2,1)S(1)} collective-permute-done((f16[4,16,1024]{2,1,0:T(8,128)(2,1)S(1)}, f16[4,16,1024]{2,1,0:T(8,128)(2,1)S(1)}, u32[]{:S(2)}, u32[]{:S(2)}) %collective-permute-start) | collective-permute-done | bytes 131104 | tf_op jit(solution)/shard_map/ppermute | solution.py:202
  8.6 3.5 %collective-permute-start.1 = (f16[4,16,1024]{2,1,0:T(8,128)(2,1)S(1)}, f16[4,16,1024]{2,1,0:T(8,128)(2,1)S(1)}, u32[]{:S(2)}, u32[]{:S(2)}) collective-permute-start(f16[4,16,1024]{2,1,0:T(8,128)(2,1)S(1)} %broadcast_select_fusion.1), channel_id=1, source_target_pairs={{0,12},{1,5},{2,14},{3,7},{4,8},{5,1},{6,10},{7,3},{8,4},{9,13},{1... | collective-permute-start | bytes 393224 | tf_op jit(solution)/shard_map/ppermute | solution.py:202
  12.1 0.0 collective-permute-done.2
  12.1 3.4 %collective-permute-start.3 = (f16[4,16,1024]{2,1,0:T(8,128)(2,1)S(1)}, f16[4,16,1024]{2,1,0:T(8,128)(2,1)S(1)}, u32[]{:S(2)}, u32[]{:S(2)}) collective-permute-start(f16[4,16,1024]{2,1,0:T(8,128)(2,1)S(1)} %broadcast_select_fusion), channel_id=1, source_target_pairs={{0,12},{1,5},{2,14},{3,7},{4,8},{5,1},{6,10},{7,3},{8,4},{9,13},{1... | collective-permute-start | bytes 393224 | tf_op jit(solution)/shard_map/ppermute | solution.py:202
  15.5 1.3 %collective-permute-done.1 = f16[4,16,1024]{2,1,0:T(8,128)(2,1)S(1)} collective-permute-done((f16[4,16,1024]{2,1,0:T(8,128)(2,1)S(1)}, f16[4,16,1024]{2,1,0:T(8,128)(2,1)S(1)}, u32[]{:S(2)}, u32[]{:S(2)}) %collective-permute-start.1) | collective-permute-done | bytes 131104 | tf_op jit(solution)/shard_map/ppermute | solution.py:202
  16.8 0.1 convert_multiply_fusion.1
  17.0 2.7 %collective-permute-done.3 = f16[4,16,1024]{2,1,0:T(8,128)(2,1)S(1)} collective-permute-done((f16[4,16,1024]{2,1,0:T(8,128)(2,1)S(1)}, f16[4,16,1024]{2,1,0:T(8,128)(2,1)S(1)}, u32[]{:S(2)}, u32[]{:S(2)}) %collective-permute-start.3) | collective-permute-done | bytes 131104 | tf_op jit(solution)/shard_map/ppermute | solution.py:202
  19.6 0.1 convert_multiply_fusion
  19.8 0.1 pad_maximum_fusion
  19.9 0.1 collective-permute-start.4
  20.0 1.6 %collective-permute-start.5 = (f16[9,2,1024]{2,1,0:T(2,128)(2,1)S(1)}, f16[9,2,1024]{2,1,0:T(2,128)(2,1)S(1)}, u32[]{:S(2)}, u32[]{:S(2)}) collective-permute-start(f16[9,2,1024]{2,1,0:T(2,128)(2,1)S(1)} %get-tuple-element.20), channel_id=1, source_target_pairs={{0,3},{1,2},{2,1},{3,0},{4,7},{5,6},{6,5},{7,4},{8,11},{9,10},{10,... | collective-permute-start | bytes 110600 | tf_op jit(solution)/shard_map/ppermute | solution.py:253
  21.6 0.9 %shard_map.46 = (f32[8,16,1024]{2,1,0:T(8,128)S(1)}, f32[8,8,1024]{2,1,0:T(8,128)S(1)}, f32[8,8,1024]{2,1,0:T(8,128)S(1)}, f32[2,8,1024]{2,1,0:T(8,128)S(1)}) custom-call(f32[4,16,1024]{2,1,0:T(8,128)S(1)} %get-tuple-element.23.refs_0_, f32[4,16,1024]{2,1,0:T(8,128)S(1)} %get-tuple-element.21.refs_1_, bf16[2,16,1024]{2,1,0:T(8,128)(2,1)S(1)} %copy.6.refs_2_), custom_call_target="tpu_custom_call" | custom-call | flops 14417920 | bytes 1048576 | tf_op jit(solution)/shard_map/pallas_call | solution.py:162
  22.5 0.0 collective-permute-done.4
  22.5 0.9 %collective-permute-done.5 = f16[9,2,1024]{2,1,0:T(2,128)(2,1)S(1)} collective-permute-done((f16[9,2,1024]{2,1,0:T(2,128)(2,1)S(1)}, f16[9,2,1024]{2,1,0:T(2,128)(2,1)S(1)}, u32[]{:S(2)}, u32[]{:S(2)}) %collective-permute-start.5) | collective-permute-done | bytes 36896 | tf_op jit(solution)/shard_map/ppermute | solution.py:253
  23.5 1.3 %shard_map.47 = f32[8,16,1024]{2,1,0:T(8,128)} custom-call(f32[8,16,1024]{2,1,0:T(8,128)S(1)} %get-tuple-element.15.inner_ref, f32[8,8,1024]{2,1,0:T(8,128)S(1)} %get-tuple-element.16.raw_ref, f32[8,8,1024]{2,1,0:T(8,128)S(1)} %get-tuple-element.17.once_ref, f32[2,8,1024]{2,1,0:T(8,128)S(1)} %get-tuple-element.18.fog_ref, ...), custom_call_target="tpu_custom_call" | custom-call | flops 7208960 | bytes 1048576 | tf_op jit(solution)/shard_map/pallas_call | solution.py:176
  (8 shorter events, 0.3 us)
Async XLA Ops:
  0.0 6.2 %copy-start = (bf16[1,2,16,1024]{3,2,1,0:T(8,128)(2,1)S(1)}, bf16[1,2,16,1024]{3,2,1,0:T(8,128)(2,1)}, u32[]{:S(2)}) copy-start(bf16[1,2,16,1024]{3,2,1,0:T(8,128)(2,1)} %param.6) | copy-start | bytes 196612
  1.1 7.4 %collective-permute-start = (f16[4,16,1024]{2,1,0:T(8,128)(2,1)S(1)}, f16[4,16,1024]{2,1,0:T(8,128)(2,1)S(1)}, u32[]{:S(2)}, u32[]{:S(2)}) collective-permute-start(f16[4,16,1024]{2,1,0:T(8,128)(2,1)S(1)} %get-tuple-element.13), channel_id=1, source_target_pairs={{0,4},{1,13},{2,6},{3,15},{4,0},{5,9},{6,2},{7,11},{8,12},{9,5},{1... | collective-permute-start | bytes 393224 | tf_op jit(solution)/shard_map/ppermute | solution.py:202
  4.2 7.9 %collective-permute-start.2 = (f16[4,16,1024]{2,1,0:T(8,128)(2,1)S(1)}, f16[4,16,1024]{2,1,0:T(8,128)(2,1)S(1)}, u32[]{:S(2)}, u32[]{:S(2)}) collective-permute-start(f16[4,16,1024]{2,1,0:T(8,128)(2,1)S(1)} %get-tuple-element.14), channel_id=1, source_target_pairs={{0,4},{1,13},{2,6},{3,15},{4,0},{5,9},{6,2},{7,11},{8,12},{9,5},{1... | collective-permute-start | bytes 393224 | tf_op jit(solution)/shard_map/ppermute | solution.py:202
  4.3 0.7 %copy-start.1 = (s32[4]{0:T(128)S(1)}, s32[4]{0:T(128)}, u32[]{:S(2)}) copy-start(s32[4]{0:T(128)} %param.5) | copy-start | bytes 52
  8.6 8.2 %collective-permute-start.1 = (f16[4,16,1024]{2,1,0:T(8,128)(2,1)S(1)}, f16[4,16,1024]{2,1,0:T(8,128)(2,1)S(1)}, u32[]{:S(2)}, u32[]{:S(2)}) collective-permute-start(f16[4,16,1024]{2,1,0:T(8,128)(2,1)S(1)} %broadcast_select_fusion.1), channel_id=1, source_target_pairs={{0,12},{1,5},{2,14},{3,7},{4,8},{5,1},{6,10},{7,3},{8,4},{9,13},{1... | collective-permute-start | bytes 393224 | tf_op jit(solution)/shard_map/ppermute | solution.py:202
  12.1 7.5 %collective-permute-start.3 = (f16[4,16,1024]{2,1,0:T(8,128)(2,1)S(1)}, f16[4,16,1024]{2,1,0:T(8,128)(2,1)S(1)}, u32[]{:S(2)}, u32[]{:S(2)}) collective-permute-start(f16[4,16,1024]{2,1,0:T(8,128)(2,1)S(1)} %broadcast_select_fusion), channel_id=1, source_target_pairs={{0,12},{1,5},{2,14},{3,7},{4,8},{5,1},{6,10},{7,3},{8,4},{9,13},{1... | collective-permute-start | bytes 393224 | tf_op jit(solution)/shard_map/ppermute | solution.py:202
  19.9 2.6 %collective-permute-start.4 = (f16[9,2,1024]{2,1,0:T(2,128)(2,1)S(1)}, f16[9,2,1024]{2,1,0:T(2,128)(2,1)S(1)}, u32[]{:S(2)}, u32[]{:S(2)}) collective-permute-start(f16[9,2,1024]{2,1,0:T(2,128)(2,1)S(1)} %get-tuple-element.19), channel_id=1, source_target_pairs={{0,1},{1,0},{2,3},{3,2},{4,5},{5,4},{6,7},{7,6},{8,9},{9,8},{10,11... | collective-permute-start | bytes 110600 | tf_op jit(solution)/shard_map/ppermute | solution.py:254
  20.0 3.4 %collective-permute-start.5 = (f16[9,2,1024]{2,1,0:T(2,128)(2,1)S(1)}, f16[9,2,1024]{2,1,0:T(2,128)(2,1)S(1)}, u32[]{:S(2)}, u32[]{:S(2)}) collective-permute-start(f16[9,2,1024]{2,1,0:T(2,128)(2,1)S(1)} %get-tuple-element.20), channel_id=1, source_target_pairs={{0,3},{1,2},{2,1},{3,0},{4,7},{5,6},{6,5},{7,4},{8,11},{9,10},{10,... | collective-permute-start | bytes 110600 | tf_op jit(solution)/shard_map/ppermute | solution.py:253

commit v4 on v3

--- a/solution.py
+++ b/solution.py
@@ -14,8 +14,10 @@
 SECOND = (1.0, 1.6)
 
 
-ACROSS = 3
-CHUNKS = 2
+PLAN = (
+    ((1, 2), (2, 1)),
+    ((1, 3), (2, 1)),
+)
 
 
 def pack(values):
@@ -192,8 +194,7 @@
 def fetch_by_permutes(state, ancestors, me, even):
     blocks = lax.axis_size("space")
 
-    def swap(a, even_mask, odd_mask):
-        masks = (even_mask, odd_mask)
+    def swap(a, masks):
         pairs = [
             (i * blocks + s, (i ^ masks[s % 2]) * blocks + s)
             for i in range(4)
@@ -201,24 +202,27 @@
         ]
         return lax.ppermute(a, ("particle", "space"), pairs)
 
-    size = state.shape[0] // CHUNKS
-    parts = [state[c * size : (c + 1) * size] for c in range(CHUNKS)]
+    def by_block(masks):
+        return jnp.where(even, *masks)
+
+    size = state.shape[0] // len(PLAN)
+    parts = [state[c * size : (c + 1) * size] for c in range(len(PLAN))]
     owns = lax.optimization_barrier([pack(p) for p in parts])
-    gots = [swap(own, 1, ACROSS) for own in owns]
+    gots = [swap(own, first) for own, (first, _) in zip(owns, PLAN)]
     places = 4 * np.arange(4, dtype=np.int32)
     code = jnp.sum(ancestors << places) ^ (me * np.sum(1 << places).astype(np.int32))
-    first = jnp.where(even, 1, ACROSS)
-    second = jnp.where(even, ACROSS, 1)
 
     def distance(slot):
         return (code >> (4 * slot)) & 3
 
-    keep = distance(me ^ second) == 0
     mine = distance(me)
     result = []
-    for own, got in zip(owns, gots):
-        last = swap(jnp.where(keep, own, got), ACROSS, 1)
-        result.append(jnp.where(mine == 0, own, jnp.where(mine == first, got, last)))
+    for own, got, (first, second) in zip(owns, gots, PLAN):
+        give = jnp.where(distance(me ^ by_block(second)) == 0, own, got)
+        last = swap(give, second)
+        result.append(
+            jnp.where(mine == 0, own, jnp.where(mine == by_block(first), got, last))
+        )
     return result
 
 

time: 24.9 us -> 23.3 us (0.936)
  the two profiles are of different devices: /device:TPU:0 before, /device:TPU:25 now
where the time goes in v4:
time: 23.3 us; the launch traced here: 23.1 us
  waiting for transfers between devices  10.3 us (44%)
  starting transfers between devices  6.87 us (29%)
  other arithmetic  2.25 us (10%)
  Pallas kernels  2.19 us (9%)
  between operations  0.79 us (3%)
  local copies, waits for them, and re-layouts  0.74 us (3%)
    ppermute x4, waiting for transfers between devices, swap(): return lax.ppermute(a, ('particle', 'space'), pairs)  9.01 us
    ppermute x4, starting transfers between devices, swap(): return lax.ppermute(a, ('particle', 'space'), pairs)  2.86 us
    ppermute x1, starting transfers between devices, per_device(): pair = lax.ppermute(to_pair, 'space', pairs)  2.84 us
    pallas_call x1, Pallas kernels, ends(): pl.pallas_call(ends_kernel, out_shape=jax.ShapeDtypeStruct((total, rows,...  1.32 us
    ppermute x1, waiting for transfers between devices, per_device(): other = lax.ppermute(to_other, 'space', others)  1.28 us
    ppermute x1, starting transfers between devices, per_device(): other = lax.ppermute(to_other, 'space', others)  1.17 us
    convert_element_type x1, other arithmetic, pack(): return (values.astype(jnp.float32) * SCALE).astype(WIRE)  1.11 us
    pallas_call x1, Pallas kernels, inner(): pl.pallas_call(functools.partial(inner_kernel, parts), out_shape=[jax.Sha...  0.87 us
  transfers between devices with their start and end apart: 6, of which 5 were waited for; matrix products, arithmetic and copies ran while one was open for 4% of the time, Pallas kernels for 4%

profile of v4, /device:TPU:25, one launch (start us, length us, event | category | flops | bytes accessed | tf_op | source)
XLA Modules:
  0.0 23.1 jit_solution(15474559174344854213)
XLA Ops:
  0.0 0.0 copy-start
  0.0 1.1 %fusion.1 = (f16[4,16,1024]{2,1,0:T(8,128)(2,1)S(1)}, f16[4,16,1024]{2,1,0:T(8,128)(2,1)S(1)}) fusion(f32[1,8,16,1024]{3,2,1,0:T(8,128)} %param.4), kind=kLoop, calls=%fused_computation.5 | loop fusion | flops 262144 | bytes 786432 | tf_op jit(solution)/shard_map/convert_element_type | solution.py:24
  1.1 0.1 collective-permute-start
  1.2 2.2 %collective-permute-start.2 = (f16[4,16,1024]{2,1,0:T(8,128)(2,1)S(1)}, f16[4,16,1024]{2,1,0:T(8,128)(2,1)S(1)}, u32[]{:S(2)}, u32[]{:S(2)}) collective-permute-start(f16[4,16,1024]{2,1,0:T(8,128)(2,1)S(1)} %get-tuple-element.14), channel_id=1, source_target_pairs={{0,4},{1,13},{2,6},{3,15},{4,0},{5,9},{6,2},{7,11},{8,12},{9,5},{1... | collective-permute-start | bytes 393224 | tf_op jit(solution)/shard_map/ppermute | solution.py:203
  3.4 0.0 copy-start.1
  3.4 0.7 %copy-done.1 = s32[4]{0:T(128)S(1)} copy-done((s32[4]{0:T(128)S(1)}, s32[4]{0:T(128)}, u32[]{:S(2)}) %copy-start.1) | copy-done | bytes 40
  4.1 0.6 %shift-left_reduce_fusion = s32[]{:T(128)} fusion(s32[4]{0:T(128)S(1)} %copy-done.1), kind=kLoop, calls=%fused_computation.23 | loop fusion | flops 11 | bytes 20 | tf_op jit(solution)/shard_map/reduce_sum | solution.py:213
  5.4 0.0 copy-done
  5.4 0.1 copy.8
  5.5 1.9 %collective-permute-done = f16[4,16,1024]{2,1,0:T(8,128)(2,1)S(1)} collective-permute-done((f16[4,16,1024]{2,1,0:T(8,128)(2,1)S(1)}, f16[4,16,1024]{2,1,0:T(8,128)(2,1)S(1)}, u32[]{:S(2)}, u32[]{:S(2)}) %collective-permute-start) | collective-permute-done | bytes 131104 | tf_op jit(solution)/shard_map/ppermute | solution.py:203
  7.5 0.1 collective-permute-start.1
  7.5 2.3 %collective-permute-done.2 = f16[4,16,1024]{2,1,0:T(8,128)(2,1)S(1)} collective-permute-done((f16[4,16,1024]{2,1,0:T(8,128)(2,1)S(1)}, f16[4,16,1024]{2,1,0:T(8,128)(2,1)S(1)}, u32[]{:S(2)}, u32[]{:S(2)}) %collective-permute-start.2) | collective-permute-done | bytes 131104 | tf_op jit(solution)/shard_map/ppermute | solution.py:203
  9.9 0.5 %collective-permute-start.3 = (f16[4,16,1024]{2,1,0:T(8,128)(2,1)S(1)}, f16[4,16,1024]{2,1,0:T(8,128)(2,1)S(1)}, u32[]{:S(2)}, u32[]{:S(2)}) collective-permute-start(f16[4,16,1024]{2,1,0:T(8,128)(2,1)S(1)} %broadcast_select_fusion), channel_id=1, source_target_pairs={{0,8},{1,5},{2,10},{3,7},{4,12},{5,1},{6,14},{7,3},{8,0},{9,13},{1... | collective-permute-start | bytes 393224 | tf_op jit(solution)/shard_map/ppermute | solution.py:203
  10.4 1.2 %collective-permute-done.1 = f16[4,16,1024]{2,1,0:T(8,128)(2,1)S(1)} collective-permute-done((f16[4,16,1024]{2,1,0:T(8,128)(2,1)S(1)}, f16[4,16,1024]{2,1,0:T(8,128)(2,1)S(1)}, u32[]{:S(2)}, u32[]{:S(2)}) %collective-permute-start.1) | collective-permute-done | bytes 131104 | tf_op jit(solution)/shard_map/ppermute | solution.py:203
  11.6 0.1 convert_multiply_fusion.1
  11.8 3.5 %collective-permute-done.3 = f16[4,16,1024]{2,1,0:T(8,128)(2,1)S(1)} collective-permute-done((f16[4,16,1024]{2,1,0:T(8,128)(2,1)S(1)}, f16[4,16,1024]{2,1,0:T(8,128)(2,1)S(1)}, u32[]{:S(2)}, u32[]{:S(2)}) %collective-permute-start.3) | collective-permute-done | bytes 131104 | tf_op jit(solution)/shard_map/ppermute | solution.py:203
  15.3 0.1 convert_multiply_fusion
  15.4 0.1 pad_maximum_fusion
  15.5 2.8 %collective-permute-start.4 = (f16[9,2,1024]{2,1,0:T(2,128)(2,1)S(1)}, f16[9,2,1024]{2,1,0:T(2,128)(2,1)S(1)}, u32[]{:S(2)}, u32[]{:S(2)}) collective-permute-start(f16[9,2,1024]{2,1,0:T(2,128)(2,1)S(1)} %get-tuple-element.19), channel_id=1, source_target_pairs={{0,1},{1,0},{2,3},{3,2},{4,5},{5,4},{6,7},{7,6},{8,9},{9,8},{10,11... | collective-permute-start | bytes 110600 | tf_op jit(solution)/shard_map/ppermute | solution.py:258
  18.4 1.2 %collective-permute-start.5 = (f16[9,2,1024]{2,1,0:T(2,128)(2,1)S(1)}, f16[9,2,1024]{2,1,0:T(2,128)(2,1)S(1)}, u32[]{:S(2)}, u32[]{:S(2)}) collective-permute-start(f16[9,2,1024]{2,1,0:T(2,128)(2,1)S(1)} %get-tuple-element.20), channel_id=1, source_target_pairs={{0,3},{1,2},{2,1},{3,0},{4,7},{5,6},{6,5},{7,4},{8,11},{9,10},{10,... | collective-permute-start | bytes 110600 | tf_op jit(solution)/shard_map/ppermute | solution.py:257
  19.6 0.9 %shard_map.46 = (f32[8,16,1024]{2,1,0:T(8,128)S(1)}, f32[8,8,1024]{2,1,0:T(8,128)S(1)}, f32[8,8,1024]{2,1,0:T(8,128)S(1)}, f32[2,8,1024]{2,1,0:T(8,128)S(1)}) custom-call(f32[4,16,1024]{2,1,0:T(8,128)S(1)} %get-tuple-element.23.refs_0_, f32[4,16,1024]{2,1,0:T(8,128)S(1)} %get-tuple-element.21.refs_1_, bf16[2,16,1024]{2,1,0:T(8,128)(2,1)S(1)} %copy.6.refs_2_), custom_call_target="tpu_custom_call" | custom-call | flops 14417920 | bytes 1048576 | tf_op jit(solution)/shard_map/pallas_call | solution.py:164
  20.5 0.0 collective-permute-done.4
  20.5 1.3 %collective-permute-done.5 = f16[9,2,1024]{2,1,0:T(2,128)(2,1)S(1)} collective-permute-done((f16[9,2,1024]{2,1,0:T(2,128)(2,1)S(1)}, f16[9,2,1024]{2,1,0:T(2,128)(2,1)S(1)}, u32[]{:S(2)}, u32[]{:S(2)}) %collective-permute-start.5) | collective-permute-done | bytes 36896 | tf_op jit(solution)/shard_map/ppermute | solution.py:257
  21.8 1.3 %shard_map.47 = f32[8,16,1024]{2,1,0:T(8,128)} custom-call(f32[8,16,1024]{2,1,0:T(8,128)S(1)} %get-tuple-element.15.inner_ref, f32[8,8,1024]{2,1,0:T(8,128)S(1)} %get-tuple-element.16.raw_ref, f32[8,8,1024]{2,1,0:T(8,128)S(1)} %get-tuple-element.17.once_ref, f32[2,8,1024]{2,1,0:T(8,128)S(1)} %get-tuple-element.18.fog_ref, ...), custom_call_target="tpu_custom_call" | custom-call | flops 7208960 | bytes 1048576 | tf_op jit(solution)/shard_map/pallas_call | solution.py:178
  (8 shorter events, 0.3 us)
Async XLA Ops:
  0.0 5.4 %copy-start = (bf16[1,2,16,1024]{3,2,1,0:T(8,128)(2,1)S(1)}, bf16[1,2,16,1024]{3,2,1,0:T(8,128)(2,1)}, u32[]{:S(2)}) copy-start(bf16[1,2,16,1024]{3,2,1,0:T(8,128)(2,1)} %param.6) | copy-start | bytes 196612
  1.1 6.3 %collective-permute-start = (f16[4,16,1024]{2,1,0:T(8,128)(2,1)S(1)}, f16[4,16,1024]{2,1,0:T(8,128)(2,1)S(1)}, u32[]{:S(2)}, u32[]{:S(2)}) collective-permute-start(f16[4,16,1024]{2,1,0:T(8,128)(2,1)S(1)} %get-tuple-element.13), channel_id=1, source_target_pairs={{0,4},{1,9},{2,6},{3,11},{4,0},{5,13},{6,2},{7,15},{8,12},{9,1},{1... | collective-permute-start | bytes 393224 | tf_op jit(solution)/shard_map/ppermute | solution.py:203
  1.2 8.6 %collective-permute-start.2 = (f16[4,16,1024]{2,1,0:T(8,128)(2,1)S(1)}, f16[4,16,1024]{2,1,0:T(8,128)(2,1)S(1)}, u32[]{:S(2)}, u32[]{:S(2)}) collective-permute-start(f16[4,16,1024]{2,1,0:T(8,128)(2,1)S(1)} %get-tuple-element.14), channel_id=1, source_target_pairs={{0,4},{1,13},{2,6},{3,15},{4,0},{5,9},{6,2},{7,11},{8,12},{9,5},{1... | collective-permute-start | bytes 393224 | tf_op jit(solution)/shard_map/ppermute | solution.py:203
  3.4 0.7 %copy-start.1 = (s32[4]{0:T(128)S(1)}, s32[4]{0:T(128)}, u32[]{:S(2)}) copy-start(s32[4]{0:T(128)} %param.5) | copy-start | bytes 52
  7.5 4.2 %collective-permute-start.1 = (f16[4,16,1024]{2,1,0:T(8,128)(2,1)S(1)}, f16[4,16,1024]{2,1,0:T(8,128)(2,1)S(1)}, u32[]{:S(2)}, u32[]{:S(2)}) collective-permute-start(f16[4,16,1024]{2,1,0:T(8,128)(2,1)S(1)} %broadcast_select_fusion.1), channel_id=1, source_target_pairs={{0,8},{1,5},{2,10},{3,7},{4,12},{5,1},{6,14},{7,3},{8,0},{9,13},{1... | collective-permute-start | bytes 393224 | tf_op jit(solution)/shard_map/ppermute | solution.py:203
  9.9 5.4 %collective-permute-start.3 = (f16[4,16,1024]{2,1,0:T(8,128)(2,1)S(1)}, f16[4,16,1024]{2,1,0:T(8,128)(2,1)S(1)}, u32[]{:S(2)}, u32[]{:S(2)}) collective-permute-start(f16[4,16,1024]{2,1,0:T(8,128)(2,1)S(1)} %broadcast_select_fusion), channel_id=1, source_target_pairs={{0,8},{1,5},{2,10},{3,7},{4,12},{5,1},{6,14},{7,3},{8,0},{9,13},{1... | collective-permute-start | bytes 393224 | tf_op jit(solution)/shard_map/ppermute | solution.py:203
  15.5 4.9 %collective-permute-start.4 = (f16[9,2,1024]{2,1,0:T(2,128)(2,1)S(1)}, f16[9,2,1024]{2,1,0:T(2,128)(2,1)S(1)}, u32[]{:S(2)}, u32[]{:S(2)}) collective-permute-start(f16[9,2,1024]{2,1,0:T(2,128)(2,1)S(1)} %get-tuple-element.19), channel_id=1, source_target_pairs={{0,1},{1,0},{2,3},{3,2},{4,5},{5,4},{6,7},{7,6},{8,9},{9,8},{10,11... | collective-permute-start | bytes 110600 | tf_op jit(solution)/shard_map/ppermute | solution.py:258
  18.4 3.4 %collective-permute-start.5 = (f16[9,2,1024]{2,1,0:T(2,128)(2,1)S(1)}, f16[9,2,1024]{2,1,0:T(2,128)(2,1)S(1)}, u32[]{:S(2)}, u32[]{:S(2)}) collective-permute-start(f16[9,2,1024]{2,1,0:T(2,128)(2,1)S(1)} %get-tuple-element.20), channel_id=1, source_target_pairs={{0,3},{1,2},{2,1},{3,0},{4,7},{5,6},{6,5},{7,4},{8,11},{9,10},{10,... | collective-permute-start | bytes 110600 | tf_op jit(solution)/shard_map/ppermute | solution.py:257

commit v5 on v4

--- a/solution.py
+++ b/solution.py
@@ -97,7 +97,7 @@
 
 
 def ends_kernel(
-    inner_ref, raw_ref, once_ref, fog_ref, pair_ref, other_ref, out_hbm, out, sems
+    inner_ref, raw_ref, once_ref, fog_ref, other_ref, pair_ref, out_hbm, out, sems
 ):
     where = lax.axis_index("space")
     even = lax.rem(where, 2) == 0
@@ -173,7 +173,7 @@
     )(*pieces, noise)
 
 
-def ends(kept, pair, other):
+def ends(kept, other, pair):
     total, rows, cols = kept[0].shape
     return pl.pallas_call(
         ends_kernel,
@@ -188,7 +188,7 @@
         cost_estimate=pl.CostEstimate(
             flops=110 * total * 8 * cols, bytes_accessed=1 << 20, transcendentals=0
         ),
-    )(*kept, pair, other)
+    )(*kept, other, pair)
 
 
 def fetch_by_permutes(state, ancestors, me, even):
@@ -207,7 +207,8 @@
 
     size = state.shape[0] // len(PLAN)
     parts = [state[c * size : (c + 1) * size] for c in range(len(PLAN))]
-    owns = lax.optimization_barrier([pack(p) for p in parts])
+    later = lax.optimization_barrier(state)[size:]
+    owns = [lax.optimization_barrier(pack(p)) for p in (parts[0], later)]
     gots = [swap(own, first) for own, (first, _) in zip(owns, PLAN)]
     places = 4 * np.arange(4, dtype=np.int32)
     code = jnp.sum(ancestors << places) ^ (me * np.sum(1 << places).astype(np.int32))
@@ -251,14 +252,14 @@
     sides = [(p[:, :2], p[:, -2:]) for p in pieces] + [(fog_low, fog_high)]
     to_pair = jnp.concatenate([jnp.where(even, h, l) for l, h in sides], axis=0)
     to_other = jnp.concatenate([jnp.where(even, l, h) for l, h in sides], axis=0)
-    to_other, to_pair = lax.optimization_barrier((to_other, to_pair))
+    to_other, to_pair, pieces = lax.optimization_barrier((to_other, to_pair, pieces))
     pairs = [(i, i ^ 1) for i in range(blocks)]
     others = [(i, (i + 1 if i % 2 else i - 1) % blocks) for i in range(blocks)]
     other = lax.ppermute(to_other, "space", others)
     pair = lax.ppermute(to_pair, "space", pairs)
 
     kept = inner([unpack(p) for p in pieces], noise)
-    out = ends(kept, pair.astype(jnp.float32), other.astype(jnp.float32))
+    out = ends(kept, other.astype(jnp.float32), pair.astype(jnp.float32))
     return out[None]
 
 

time: 23.3 us -> 22.9 us (0.983)
  the two profiles are of different devices: /device:TPU:25 before, /device:TPU:0 now
where the time goes in v5:
time: 22.9 us; the launch traced here: 22.7 us
  starting transfers between devices  9.91 us (43%)
  waiting for transfers between devices  5.92 us (26%)
  other arithmetic  3.16 us (14%)
  Pallas kernels  2.19 us (10%)
  between operations  0.8 us (3%)
  local copies, waits for them, and re-layouts  0.74 us (3%)
    ppermute x4, starting transfers between devices, swap(): return lax.ppermute(a, ('particle', 'space'), pairs)  8.24 us
    ppermute x4, waiting for transfers between devices, swap(): return lax.ppermute(a, ('particle', 'space'), pairs)  4.9 us
    convert_element_type x2, other arithmetic, pack(): return (values.astype(jnp.float32) * SCALE).astype(WIRE)  1.98 us
    pallas_call x1, Pallas kernels, ends(): pl.pallas_call(ends_kernel, out_shape=jax.ShapeDtypeStruct((total, rows,...  1.31 us
    ppermute x1, starting transfers between devices, per_device(): other = lax.ppermute(to_other, 'space', others)  1.22 us
    ppermute x1, waiting for transfers between devices, per_device(): other = lax.ppermute(to_other, 'space', others)  1.02 us
    pallas_call x1, Pallas kernels, inner(): pl.pallas_call(functools.partial(inner_kernel, parts), out_shape=[jax.Sha...  0.87 us
    unnamed x5, local copies, waits for them, and re-layouts  0.72 us
  transfers between devices with their start and end apart: 6, of which 5 were waited for; matrix products, arithmetic and copies ran while one was open for 9% of the time, Pallas kernels for 4%

profile of v5, /device:TPU:0, one launch (start us, length us, event | category | flops | bytes accessed | tf_op | source)
XLA Modules:
  0.0 22.7 jit_solution(16142751647611510270)
XLA Ops:
  0.0 1.0 %fusion.1 = f16[4,16,1024]{2,1,0:T(8,128)(2,1)S(1)} fusion(f32[1,8,16,1024]{3,2,1,0:T(8,128)} %param.4), kind=kLoop, calls=%fused_computation.5 | loop fusion | flops 131072 | bytes 393216 | tf_op jit(solution)/shard_map/convert_element_type | solution.py:24
  1.0 3.1 %collective-permute-start = (f16[4,16,1024]{2,1,0:T(8,128)(2,1)S(1)}, f16[4,16,1024]{2,1,0:T(8,128)(2,1)S(1)}, u32[]{:S(2)}, u32[]{:S(2)}) collective-permute-start(f16[4,16,1024]{2,1,0:T(8,128)(2,1)S(1)} %fusion.1), channel_id=1, source_target_pairs={{0,4},{1,9},{2,6},{3,11},{4,0},{5,13},{6,2},{7,15},{8,12},{9,1},{1... | collective-permute-start | bytes 393224 | tf_op jit(solution)/shard_map/ppermute | solution.py:203
  4.1 1.0 %fusion = f16[4,16,1024]{2,1,0:T(8,128)(2,1)S(1)} fusion(f32[8,16,1024]{2,1,0:T(8,128)} %bitcast.11), kind=kLoop, calls=%fused_computation.1 | loop fusion | flops 131072 | bytes 393216 | tf_op jit(solution)/shard_map/convert_element_type | solution.py:24
  5.1 0.1 collective-permute-start.2
  5.2 0.0 copy-start.1
  5.2 0.6 %copy-done.1 = s32[4]{0:T(128)S(1)} copy-done((s32[4]{0:T(128)S(1)}, s32[4]{0:T(128)}, u32[]{:S(2)}) %copy-start.1) | copy-done | bytes 40
  5.8 0.6 %shift-left_reduce_fusion = s32[]{:T(128)} fusion(s32[4]{0:T(128)S(1)} %copy-done.1), kind=kLoop, calls=%fused_computation.23 | loop fusion | flops 11 | bytes 20 | tf_op jit(solution)/shard_map/reduce_sum | solution.py:214
  7.1 0.0 copy-done
  7.1 0.1 copy.8
  7.3 0.9 %collective-permute-done = f16[4,16,1024]{2,1,0:T(8,128)(2,1)S(1)} collective-permute-done((f16[4,16,1024]{2,1,0:T(8,128)(2,1)S(1)}, f16[4,16,1024]{2,1,0:T(8,128)(2,1)S(1)}, u32[]{:S(2)}, u32[]{:S(2)}) %collective-permute-start) | collective-permute-done | bytes 131104 | tf_op jit(solution)/shard_map/ppermute | solution.py:203
  8.2 2.3 %collective-permute-start.1 = (f16[4,16,1024]{2,1,0:T(8,128)(2,1)S(1)}, f16[4,16,1024]{2,1,0:T(8,128)(2,1)S(1)}, u32[]{:S(2)}, u32[]{:S(2)}) collective-permute-start(f16[4,16,1024]{2,1,0:T(8,128)(2,1)S(1)} %broadcast_select_fusion.1), channel_id=1, source_target_pairs={{0,8},{1,5},{2,10},{3,7},{4,12},{5,1},{6,14},{7,3},{8,0},{9,13},{1... | collective-permute-start | bytes 393224 | tf_op jit(solution)/shard_map/ppermute | solution.py:203
  10.5 0.3 %collective-permute-done.2 = f16[4,16,1024]{2,1,0:T(8,128)(2,1)S(1)} collective-permute-done((f16[4,16,1024]{2,1,0:T(8,128)(2,1)S(1)}, f16[4,16,1024]{2,1,0:T(8,128)(2,1)S(1)}, u32[]{:S(2)}, u32[]{:S(2)}) %collective-permute-start.2) | collective-permute-done | bytes 131104 | tf_op jit(solution)/shard_map/ppermute | solution.py:203
  10.8 2.8 %collective-permute-start.3 = (f16[4,16,1024]{2,1,0:T(8,128)(2,1)S(1)}, f16[4,16,1024]{2,1,0:T(8,128)(2,1)S(1)}, u32[]{:S(2)}, u32[]{:S(2)}) collective-permute-start(f16[4,16,1024]{2,1,0:T(8,128)(2,1)S(1)} %broadcast_select_fusion), channel_id=1, source_target_pairs={{0,8},{1,5},{2,10},{3,7},{4,12},{5,1},{6,14},{7,3},{8,0},{9,13},{1... | collective-permute-start | bytes 393224 | tf_op jit(solution)/shard_map/ppermute | solution.py:203
  13.6 0.6 %collective-permute-done.1 = f16[4,16,1024]{2,1,0:T(8,128)(2,1)S(1)} collective-permute-done((f16[4,16,1024]{2,1,0:T(8,128)(2,1)S(1)}, f16[4,16,1024]{2,1,0:T(8,128)(2,1)S(1)}, u32[]{:S(2)}, u32[]{:S(2)}) %collective-permute-start.1) | collective-permute-done | bytes 131104 | tf_op jit(solution)/shard_map/ppermute | solution.py:203
  14.2 0.1 select_select_fusion.1
  14.3 3.1 %collective-permute-done.3 = f16[4,16,1024]{2,1,0:T(8,128)(2,1)S(1)} collective-permute-done((f16[4,16,1024]{2,1,0:T(8,128)(2,1)S(1)}, f16[4,16,1024]{2,1,0:T(8,128)(2,1)S(1)}, u32[]{:S(2)}, u32[]{:S(2)}) %collective-permute-start.3) | collective-permute-done | bytes 131104 | tf_op jit(solution)/shard_map/ppermute | solution.py:203
  17.4 0.1 select_select_fusion
  17.6 0.1 pad_maximum_fusion
  17.7 1.2 %collective-permute-start.4 = (f16[9,2,1024]{2,1,0:T(2,128)(2,1)S(1)}, f16[9,2,1024]{2,1,0:T(2,128)(2,1)S(1)}, u32[]{:S(2)}, u32[]{:S(2)}) collective-permute-start(f16[9,2,1024]{2,1,0:T(2,128)(2,1)S(1)} %get-tuple-element.19), channel_id=1, source_target_pairs={{0,3},{1,2},{2,1},{3,0},{4,7},{5,6},{6,5},{7,4},{8,11},{9,10},{10,... | collective-permute-start | bytes 110600 | tf_op jit(solution)/shard_map/ppermute | solution.py:258
  18.9 0.5 %collective-permute-start.5 = (f16[9,2,1024]{2,1,0:T(2,128)(2,1)S(1)}, f16[9,2,1024]{2,1,0:T(2,128)(2,1)S(1)}, u32[]{:S(2)}, u32[]{:S(2)}) collective-permute-start(f16[9,2,1024]{2,1,0:T(2,128)(2,1)S(1)} %get-tuple-element.20), channel_id=1, source_target_pairs={{0,1},{1,0},{2,3},{3,2},{4,5},{5,4},{6,7},{7,6},{8,9},{9,8},{10,11... | collective-permute-start | bytes 110600 | tf_op jit(solution)/shard_map/ppermute | solution.py:259
  19.4 0.9 %shard_map.46 = (f32[8,16,1024]{2,1,0:T(8,128)S(1)}, f32[8,8,1024]{2,1,0:T(8,128)S(1)}, f32[8,8,1024]{2,1,0:T(8,128)S(1)}, f32[2,8,1024]{2,1,0:T(8,128)S(1)}) custom-call(f32[4,16,1024]{2,1,0:T(8,128)S(1)} %convert_multiply_fusion.1.refs_0_, f32[4,16,1024]{2,1,0:T(8,128)S(1)} %convert_multiply_fusion.refs_1_, bf16[2,16,1024]{2,1,0:T(8,128)(2,1)S(1)} %copy.6.refs_2_), custom_call_target="tpu_custom_call" | custom-call | flops 14417920 | bytes 1048576 | tf_op jit(solution)/shard_map/pallas_call | solution.py:164
  20.3 1.0 %collective-permute-done.4 = f16[9,2,1024]{2,1,0:T(2,128)(2,1)S(1)} collective-permute-done((f16[9,2,1024]{2,1,0:T(2,128)(2,1)S(1)}, f16[9,2,1024]{2,1,0:T(2,128)(2,1)S(1)}, u32[]{:S(2)}, u32[]{:S(2)}) %collective-permute-start.4) | collective-permute-done | bytes 36896 | tf_op jit(solution)/shard_map/ppermute | solution.py:258
  21.4 0.0 collective-permute-done.5
  21.4 1.3 %shard_map.47 = f32[8,16,1024]{2,1,0:T(8,128)} custom-call(f32[8,16,1024]{2,1,0:T(8,128)S(1)} %get-tuple-element.15.inner_ref, f32[8,8,1024]{2,1,0:T(8,128)S(1)} %get-tuple-element.16.raw_ref, f32[8,8,1024]{2,1,0:T(8,128)S(1)} %get-tuple-element.17.once_ref, f32[2,8,1024]{2,1,0:T(8,128)S(1)} %get-tuple-element.18.fog_ref, ...), custom_call_target="tpu_custom_call" | custom-call | flops 7208960 | bytes 1048576 | tf_op jit(solution)/shard_map/pallas_call | solution.py:178
  (11 shorter events, 0.3 us)
Async XLA Ops:
  1.0 7.2 %collective-permute-start = (f16[4,16,1024]{2,1,0:T(8,128)(2,1)S(1)}, f16[4,16,1024]{2,1,0:T(8,128)(2,1)S(1)}, u32[]{:S(2)}, u32[]{:S(2)}) collective-permute-start(f16[4,16,1024]{2,1,0:T(8,128)(2,1)S(1)} %fusion.1), channel_id=1, source_target_pairs={{0,4},{1,9},{2,6},{3,11},{4,0},{5,13},{6,2},{7,15},{8,12},{9,1},{1... | collective-permute-start | bytes 393224 | tf_op jit(solution)/shard_map/ppermute | solution.py:203
  4.1 3.1 %copy-start = (bf16[1,2,16,1024]{3,2,1,0:T(8,128)(2,1)S(1)}, bf16[1,2,16,1024]{3,2,1,0:T(8,128)(2,1)}, u32[]{:S(2)}) copy-start(bf16[1,2,16,1024]{3,2,1,0:T(8,128)(2,1)} %param.6) | copy-start | bytes 196612
  5.1 5.7 %collective-permute-start.2 = (f16[4,16,1024]{2,1,0:T(8,128)(2,1)S(1)}, f16[4,16,1024]{2,1,0:T(8,128)(2,1)S(1)}, u32[]{:S(2)}, u32[]{:S(2)}) collective-permute-start(f16[4,16,1024]{2,1,0:T(8,128)(2,1)S(1)} %fusion), channel_id=1, source_target_pairs={{0,4},{1,13},{2,6},{3,15},{4,0},{5,9},{6,2},{7,11},{8,12},{9,5},{1... | collective-permute-start | bytes 393224 | tf_op jit(solution)/shard_map/ppermute | solution.py:203
  5.2 0.7 %copy-start.1 = (s32[4]{0:T(128)S(1)}, s32[4]{0:T(128)}, u32[]{:S(2)}) copy-start(s32[4]{0:T(128)} %param.5) | copy-start | bytes 52
  8.2 6.0 %collective-permute-start.1 = (f16[4,16,1024]{2,1,0:T(8,128)(2,1)S(1)}, f16[4,16,1024]{2,1,0:T(8,128)(2,1)S(1)}, u32[]{:S(2)}, u32[]{:S(2)}) collective-permute-start(f16[4,16,1024]{2,1,0:T(8,128)(2,1)S(1)} %broadcast_select_fusion.1), channel_id=1, source_target_pairs={{0,8},{1,5},{2,10},{3,7},{4,12},{5,1},{6,14},{7,3},{8,0},{9,13},{1... | collective-permute-start | bytes 393224 | tf_op jit(solution)/shard_map/ppermute | solution.py:203
  10.8 6.6 %collective-permute-start.3 = (f16[4,16,1024]{2,1,0:T(8,128)(2,1)S(1)}, f16[4,16,1024]{2,1,0:T(8,128)(2,1)S(1)}, u32[]{:S(2)}, u32[]{:S(2)}) collective-permute-start(f16[4,16,1024]{2,1,0:T(8,128)(2,1)S(1)} %broadcast_select_fusion), channel_id=1, source_target_pairs={{0,8},{1,5},{2,10},{3,7},{4,12},{5,1},{6,14},{7,3},{8,0},{9,13},{1... | collective-permute-start | bytes 393224 | tf_op jit(solution)/shard_map/ppermute | solution.py:203
  17.7 3.6 %collective-permute-start.4 = (f16[9,2,1024]{2,1,0:T(2,128)(2,1)S(1)}, f16[9,2,1024]{2,1,0:T(2,128)(2,1)S(1)}, u32[]{:S(2)}, u32[]{:S(2)}) collective-permute-start(f16[9,2,1024]{2,1,0:T(2,128)(2,1)S(1)} %get-tuple-element.19), channel_id=1, source_target_pairs={{0,3},{1,2},{2,1},{3,0},{4,7},{5,6},{6,5},{7,4},{8,11},{9,10},{10,... | collective-permute-start | bytes 110600 | tf_op jit(solution)/shard_map/ppermute | solution.py:258
  18.9 2.4 %collective-permute-start.5 = (f16[9,2,1024]{2,1,0:T(2,128)(2,1)S(1)}, f16[9,2,1024]{2,1,0:T(2,128)(2,1)S(1)}, u32[]{:S(2)}, u32[]{:S(2)}) collective-permute-start(f16[9,2,1024]{2,1,0:T(2,128)(2,1)S(1)} %get-tuple-element.20), channel_id=1, source_target_pairs={{0,1},{1,0},{2,3},{3,2},{4,5},{5,4},{6,7},{7,6},{8,9},{9,8},{10,11... | collective-permute-start | bytes 110600 | tf_op jit(solution)/shard_map/ppermute | solution.py:259
